TPU v7x, 32 devices: a whole 2x2x4 slice. The times are simulated.
32 devices in a mesh: ctx: 8 (over z, x), kvh: 4 (over y, core).
Axes of the slice: x: 2, y: 2, z: 4, core: 2. Of those that a mesh axis runs over, the one named last changes fastest.
Arguments:
- queries: bfloat16 [1024, 4096], P('ctx', 'kvh'), may hold values from -6 to 6
- keys: bfloat16 [1024, 512], P('ctx', 'kvh'), may hold values from -6 to 6
- values: bfloat16 [1024, 512], P('ctx', 'kvh'), may hold values from -6 to 6
- upstream: bfloat16 [1024, 4096], P('ctx', 'kvh'), may hold values from -6 to 6
- selected: int32 [8, 8], P('ctx'), may hold values from -1 to 14, as said below
- counts: int32 [8], P('ctx'), may hold values from 1 to 4, as said below
Outputs:
- attention: bfloat16 [1024, 4096], P('ctx', 'kvh')
- grad_queries: bfloat16 [1024, 4096], P(('ctx', 'kvh'))
- grad_keys: float32 [1024, 512], P('ctx', 'kvh')
- grad_values: float32 [1024, 512], P('ctx', 'kvh')
Inputs may be any that keep to these rules, and one draw needn't show every extreme that they name: `selected`: slot 0 of query block b is key block 2 b. Slot j >= 1 names one of the 2 key blocks held by the index of ctx that lies 2 ** (j - 1) below the index holding query block b, or is -1 where that index would be negative. counts[b] is at most 1 plus the number of non-negative remote slots of query block b; all slots j < counts[b] are non-negative.
All inputs are finite; a program needn't handle non-finite values.
Results may differ from a plain program's by a relative error of at most 0.04.
Values may be sent and summed in bfloat16 or wider, within the bound.
A program may use at most 64 MiB of HBM per device.

v0:
```python
import math

import jax
import jax.numpy as jnp
from jax import lax
from jax.sharding import PartitionSpec as P

HD = 128
GROUP = 8
KBLK = 64
QBLK = 128
SLOTS = 8


def from_behind(value, axis, steps):
    count = lax.axis_size(axis)
    initial, last = (max(0, -steps), min(count, count - steps))
    return lax.ppermute(value, axis, [(source, source + steps) for source in range(initial, last)])


def on_device(queries, keys, values, upstream, selected, counts):
    score_scale = 1.0 / math.sqrt(HD)
    ctx_count = lax.axis_size("ctx")
    own_index = lax.axis_index("ctx")
    blocks_here = selected.shape[0]
    key_blocks = keys.shape[0] // KBLK
    joined = jnp.concatenate([keys, values], axis=1)
    blocks_local = joined.reshape(key_blocks, KBLK, 2 * HD)
    block_range = jnp.arange(key_blocks, dtype=jnp.int32)
    everyone = lax.all_gather(selected, "ctx", axis=0, tiled=True).reshape(
        ctx_count, blocks_here, SLOTS
    )
    distances = [1 << section for section in range(SLOTS - 1) if 1 << section < ctx_count]
    askers = [
        lax.dynamic_index_in_dim(
            everyone, jnp.minimum(own_index + distance, ctx_count - 1), 0, keepdims=False
        )
        for distance in distances
    ]
    pieces = [blocks_local.reshape(blocks_here, 2, KBLK, 2 * HD)[:, 0]]
    for section, distance in enumerate(distances):
        wanted_index = askers[section][:, section + 1] - own_index * key_blocks
        pick_table = (wanted_index[:, None] == block_range[None, :]).astype(jnp.bfloat16)
        outgoing = jnp.einsum(
            "ab,btc->atc", pick_table, blocks_local, preferred_element_type=jnp.float32
        ).astype(jnp.bfloat16)
        arrived = from_behind(outgoing, "ctx", distance)
        pieces.append(arrived)
    empty_slot = jnp.zeros((blocks_here, KBLK, 2 * HD), jnp.bfloat16)
    pieces = pieces + [empty_slot] * (SLOTS - len(pieces))
    fetched = jnp.stack(pieces, axis=1)
    key_rows = fetched[..., :HD].reshape(blocks_here, SLOTS * KBLK, HD)
    value_rows = fetched[..., HD:].reshape(blocks_here, SLOTS * KBLK, HD)
    query_heads = queries.reshape(blocks_here, QBLK, GROUP, HD)
    grad_heads = upstream.reshape(blocks_here, QBLK, GROUP, HD)
    scores = (
        jnp.einsum("aihd,asd->ahis", query_heads, key_rows, preferred_element_type=jnp.float32)
        * score_scale
    )
    slot_index = jnp.arange(SLOTS * KBLK, dtype=jnp.int32) // KBLK
    offsets = jnp.arange(SLOTS * KBLK, dtype=jnp.int32) % KBLK
    key_pos = selected[:, slot_index] * KBLK + offsets
    block_ids = own_index * blocks_here + jnp.arange(blocks_here, dtype=jnp.int32)
    query_pos = block_ids[:, None] * QBLK + jnp.arange(QBLK, dtype=jnp.int32)
    live_slots = (slot_index[None, :] < counts[:, None])[:, None, :]
    visible = live_slots & (key_pos[:, None, :] <= query_pos[:, :, None])
    scores = jnp.where(visible[:, None], scores, jnp.float32(-1e30))
    peak = jnp.max(scores, axis=-1, keepdims=True)
    expon = jnp.exp(scores - peak)
    prob = expon / jnp.sum(expon, axis=-1, keepdims=True)
    prob_half = prob.astype(jnp.bfloat16)
    attended = jnp.einsum(
        "ahis,asd->aihd", prob_half, value_rows, preferred_element_type=jnp.float32
    ).astype(jnp.bfloat16)
    grad_probs = jnp.einsum(
        "aihd,asd->ahis", grad_heads, value_rows, preferred_element_type=jnp.float32
    )
    row_term = jnp.sum(grad_heads.astype(jnp.float32) * attended.astype(jnp.float32), axis=-1)
    row_term = jnp.transpose(row_term, (0, 2, 1))[..., None]
    grad_scores = (prob * (grad_probs - row_term) * score_scale).astype(jnp.bfloat16)
    grad_query = jnp.einsum(
        "ahis,asd->aihd", grad_scores, key_rows, preferred_element_type=jnp.float32
    ).astype(jnp.bfloat16)
    key_term = jnp.einsum(
        "ahis,aihd->asd", grad_scores, query_heads, preferred_element_type=jnp.float32
    )
    value_term = jnp.einsum(
        "ahis,aihd->asd", prob_half, grad_heads, preferred_element_type=jnp.float32
    )
    both_terms = jnp.concatenate([key_term, value_term], axis=-1).reshape(
        blocks_here, SLOTS, KBLK, 2 * HD
    )
    remote_sum = jnp.zeros((key_blocks, KBLK, 2 * HD), jnp.float32)
    for section, distance in enumerate(distances):
        outgoing_terms = both_terms[:, section + 1]
        arrived_terms = from_behind(outgoing_terms.astype(jnp.bfloat16), "ctx", -distance).astype(
            outgoing_terms.dtype
        )
        target_index = askers[section][:, section + 1] - own_index * key_blocks
        place_table = (target_index[:, None] == block_range[None, :]).astype(jnp.float32)
        remote_sum = remote_sum + jnp.einsum(
            "ab,atc->btc", place_table, arrived_terms, precision=lax.Precision.HIGHEST
        )
    own_terms = jnp.stack([both_terms[:, 0], jnp.zeros_like(both_terms[:, 0])], axis=1).reshape(
        key_blocks, KBLK, 2 * HD
    )
    total = (own_terms + remote_sum).reshape(key_blocks * KBLK, 2 * HD)
    grad_flat = grad_query.reshape(blocks_here * QBLK, GROUP * HD)
    grad_tokens = lax.all_to_all(grad_flat, "kvh", split_axis=0, concat_axis=1, tiled=True)
    attention = attended.reshape(blocks_here * QBLK, GROUP * HD)
    return (attention, grad_tokens, total[:, :HD], total[:, HD:])


def solution(mesh):
    placed = (
        P("ctx", "kvh"),
        P("ctx", "kvh"),
        P("ctx", "kvh"),
        P("ctx", "kvh"),
        P("ctx", None),
        P("ctx"),
    )
    return jax.shard_map(
        on_device,
        mesh=mesh,
        in_specs=placed,
        out_specs=(P("ctx", "kvh"), P(("ctx", "kvh"), None), P("ctx", "kvh"), P("ctx", "kvh")),
        check_vma=False,
    )
```

profile of v0, /device:TPU:28, one launch (start us, length us, event | category | flops | bytes accessed | tf_op | source)
XLA Modules:
  0.0 64.3 jit_solution(5743357793482097453)
XLA Ops:
  0.6 0.0 copy-start.1
  0.6 0.0 copy-start
  0.7 0.8 %constant_dynamic-update-slice_fusion.1 = bf16[128,256]{1,0:T(8,128)(2,1)S(1)} fusion(bf16[128,128]{1,0:T(8,128)(2,1)} %param.7), kind=kLoop, calls=%fused_computation.50 | loop fusion | bytes 65536
  1.5 16.0 %all-gather = s32[8,1,8]{2,1,0:T(1,128)S(1)} all-gather(s32[1,1,8]{2,1,0:T(1,128)} %bitcast.209), channel_id=1, replica_groups=mesh['ctx'=8,'kvh'=4] {'ctx'}, dimensions={0}, use_global_device_ids=true | all-gather | bytes 288 | tf_op jit(solution)/shard_map/all_gather | solution.py:30
  17.5 0.6 slice.44
  18.1 0.8 %constant_dynamic-update-slice_fusion = bf16[128,256]{1,0:T(8,128)(2,1)S(1)} fusion(bf16[128,256]{1,0:T(8,128)(2,1)S(1)} %constant_dynamic-update-slice_fusion.1, bf16[128,128]{1,0:T(8,128)(2,1)} %param.8), kind=kLoop, calls=%fused_computation.49 | loop fusion | bytes 65536 | tf_op jit(solution)/shard_map/concatenate | solution.py:27
  19.5 0.2 fusion.31
  19.7 3.5 %collective-permute-start = (bf16[1,64,256]{2,1,0:T(8,128)(2,1)S(1)}, bf16[1,64,256]{2,1,0:T(8,128)(2,1)S(1)}, u32[]{:S(2)}, u32[]{:S(2)}) collective-permute-start(bf16[1,64,256]{2,1,0:T(8,128)(2,1)S(1)} %copy.111), channel_id=1, source_target_pairs={{0,4},{4,8},{8,12},{12,16},{16,20},{20,24},{24,28},{1,5},{5,9},{9,... | collective-permute-start | bytes 98312 | tf_op jit(solution)/shard_map/ppermute | solution.py:18
  23.2 0.6 slice.45
  24.5 0.2 fusion.29
  24.7 1.3 %collective-permute-start.1 = (bf16[1,64,256]{2,1,0:T(8,128)(2,1)S(1)}, bf16[1,64,256]{2,1,0:T(8,128)(2,1)S(1)}, u32[]{:S(2)}, u32[]{:S(2)}) collective-permute-start(bf16[1,64,256]{2,1,0:T(8,128)(2,1)S(1)} %copy.112), channel_id=1, source_target_pairs={{0,8},{4,12},{8,16},{12,20},{16,24},{20,28},{1,9},{5,13},{9,17},{1... | collective-permute-start | bytes 98312 | tf_op jit(solution)/shard_map/ppermute | solution.py:18
  26.0 0.6 slice.46
  27.2 0.2 fusion.27
  27.4 1.3 %collective-permute-start.2 = (bf16[1,64,256]{2,1,0:T(8,128)(2,1)S(1)}, bf16[1,64,256]{2,1,0:T(8,128)(2,1)S(1)}, u32[]{:S(2)}, u32[]{:S(2)}) collective-permute-start(bf16[1,64,256]{2,1,0:T(8,128)(2,1)S(1)} %copy.113), channel_id=1, source_target_pairs={{0,16},{4,20},{8,24},{12,28},{1,17},{5,21},{9,25},{13,29},{2,18},{... | collective-permute-start | bytes 98312 | tf_op jit(solution)/shard_map/ppermute | solution.py:18
  28.8 1.6 %fusion.55 = (s32[1,1]{1,0:T(1,128)}, s32[1,1]{1,0:T(1,128)}, s32[1,1]{1,0:T(1,128)}, s32[1,1]{1,0:T(1,128)}, s32[1,1]{1,0:T(1,128)}, /*index=5*/s32[1,1]{1,0:T(1,128)}, s32[1,1]{1,0:T(1,128)}, s32[1,1]{1,0:T(1,128)}) fusion(s32[1,8]{1,0:T(1,128)} %param.10), kind=kLoop, calls=%fused_computation.106 | loop fusion | bytes 64 | tf_op jit(solution)/shard_map/gather | solution.py:62
  31.1 4.4 %compare_select_fusion.1 = s32[512,1]{0,1:T(1,128)S(1)} fusion(s32[]{:T(128)} %bitcast.32, s32[]{:T(128)} %bitcast.33, s32[]{:T(128)} %bitcast.34, s32[]{:T(128)} %bitcast.35, s32[]{:T(128)} %bitcast.36, s32[]{:T(128)} %bitcast.38, s32[]{:T(128)} %bitcast.37), kind=kLoop, calls=%fused_computation.53 | loop fusion | flops 11776 | bytes 2076 | tf_op jit(solution)/shard_map/gather | solution.py:62
  35.6 0.7 %fusion.34 = s32[512]{0:T(512)S(1)} fusion(pred[512]{0:T(512)(128)(4,1)S(1)} %compare_reduce_fusion, s32[512]{0:T(512)S(1)} %bitcast.210, s32[]{:T(128)} %bitcast.31), kind=kLoop, calls=%fused_computation.78 | loop fusion | flops 4608 | bytes 4612 | tf_op jit(solution)/shard_map/add | solution.py:62
  36.2 0.2 compare_and_fusion
  36.4 1.1 %copy.53 = f32[128,1024]{0,1:T(8,128)S(1)} copy(bf16[128,1024]{1,0:T(8,128)(2,1)} %param.9) | data formatting | bytes 786432 | tf_op jit(solution)/shard_map/convert_element_type | solution.py:78
  37.5 0.0 copy-done
  37.6 0.0 copy-done.1
  37.7 0.0 collective-permute-done
  37.7 0.0 collective-permute-done.1
  37.7 0.0 collective-permute-done.2
  37.7 0.1 fusion.53
  37.8 0.5 fusion.56
  38.3 0.3 fusion.4
  38.6 0.4 fusion.8
  38.9 0.3 multiply_reduce_fusion
  39.3 0.7 %fusion.2 = bf16[1,8,128,512]{2,3,1,0:T(8,128)(2,1)S(1)} fusion(bf16[512,128,1]{1,0,2:T(8,128)(2,1)S(1)} %bitcast.203, f32[8,128]{1,0:T(8,128)S(1)} %bitcast.211, f32[8,128]{1,0:T(8,128)S(1)} %fusion.4, f32[1,8,128,512]{2,3,1,0:T(8,128)S(1)} %get-tuple-element.39, f32[8,128]{1,0:T(8,128)S(1)} %get-tuple-element.38, bf16[128,1024]{1,0:T(8,128)(2,1)S(1)} %copy-done.1), kind=kOutput, calls=%fused_computation.3 | convolution fusion | flops 137363456 | bytes 3551232 | tf_op jit(solution)/shard_map/aihd,asd->ahis/dot_general | solution.py:75
  40.0 0.4 convolution_bitcast_fusion.1
  40.4 0.4 convolution_bitcast_fusion
  40.9 0.0 copy-start.2
  40.9 5.5 %collective-permute-start.5 = (bf16[1,64,256]{2,1,0:T(8,128)(2,1)S(1)}, bf16[1,64,256]{2,1,0:T(8,128)(2,1)S(1)}, u32[]{:S(2)}, u32[]{:S(2)}) collective-permute-start(bf16[1,64,256]{2,1,0:T(8,128)(2,1)S(1)} %get-tuple-element.21), channel_id=1, source_target_pairs={{16,0},{20,4},{24,8},{28,12},{17,1},{21,5},{25,9},{29,13},{18,2},{... | collective-permute-start | bytes 98312 | tf_op jit(solution)/shard_map/ppermute | solution.py:18
  46.4 0.3 fusion.5
  46.7 0.9 %copy.60 = bf16[128,1024]{1,0:T(8,128)(2,1)} copy(bf16[128,1024]{0,1:T(8,128)(2,1)S(1)} %bitcast.197) | data formatting | bytes 524288
  47.6 0.2 copy.56
  47.8 0.8 %all_to_all.14 = bf16[4,32,1024]{2,1,0:T(8,128)(2,1)} reshape(bf16[1,128,8,128]{3,2,1,0:T(8,128)(2,1)S(1)} %copy.56) | data formatting | bytes 524288 | tf_op jit(solution)/shard_map/all_to_all | solution.py:109
  48.6 3.9 %all-to-all-start = ((bf16[4,32,1024]{2,1,0:T(8,128)(2,1)}), bf16[4,32,1024]{2,1,0:T(8,128)(2,1)S(1)}, u32[]{:S(2)}, u32[]{:S(2)}) async-start(bf16[4,32,1024]{2,1,0:T(8,128)(2,1)} %all_to_all.14), calls=%async_computation | async-start | bytes 524288 | tf_op jit(solution)/shard_map/all_to_all | solution.py:109
  52.5 4.5 %collective-permute-start.4 = (bf16[1,64,256]{2,1,0:T(8,128)(2,1)S(1)}, bf16[1,64,256]{2,1,0:T(8,128)(2,1)S(1)}, u32[]{:S(2)}, u32[]{:S(2)}) collective-permute-start(bf16[1,64,256]{2,1,0:T(8,128)(2,1)S(1)} %get-tuple-element.22), channel_id=1, source_target_pairs={{8,0},{12,4},{16,8},{20,12},{24,16},{28,20},{9,1},{13,5},{17,9},{2... | collective-permute-start | bytes 98312 | tf_op jit(solution)/shard_map/ppermute | solution.py:18
  57.0 1.9 %collective-permute-start.3 = (bf16[1,64,256]{2,1,0:T(8,128)(2,1)S(1)}, bf16[1,64,256]{2,1,0:T(8,128)(2,1)S(1)}, u32[]{:S(2)}, u32[]{:S(2)}) collective-permute-start(bf16[1,64,256]{2,1,0:T(8,128)(2,1)S(1)} %get-tuple-element.20), channel_id=1, source_target_pairs={{4,0},{8,4},{12,8},{16,12},{20,16},{24,20},{28,24},{5,1},{9,5},{13... | collective-permute-start | bytes 98312 | tf_op jit(solution)/shard_map/ppermute | solution.py:18
  58.9 0.0 collective-permute-done.5
  59.0 0.0 collective-permute-done.4
  59.0 3.8 %collective-permute-done.3 = bf16[1,64,256]{2,1,0:T(8,128)(2,1)S(1)} collective-permute-done((bf16[1,64,256]{2,1,0:T(8,128)(2,1)S(1)}, bf16[1,64,256]{2,1,0:T(8,128)(2,1)S(1)}, u32[]{:S(2)}, u32[]{:S(2)}) %collective-permute-start.3) | collective-permute-done | bytes 32800 | tf_op jit(solution)/shard_map/ppermute | solution.py:18
  62.8 0.0 copy-done.2
  62.8 0.1 fusion.19
  63.0 0.7 %fusion.54 = (f32[128,128]{1,0:T(8,128)}, f32[128,128]{1,0:T(8,128)}) fusion(f32[128,256]{1,0:T(8,128)S(1)} %bitcast.201), kind=kLoop, calls=%fused_computation.105 | loop fusion | bytes 262144 | tf_op jit(solution)/shard_map/slice | solution.py:111
  63.6 0.0 all-to-all-done
  63.6 0.7 %copy.79 = bf16[4,4,8,1024]{3,2,0,1:T(8,128)(2,1)} copy(bf16[4,4,8,1024]{3,2,1,0:T(8,128)(2,1)S(1)} %bitcast.198) | data formatting | bytes 524288 | tf_op jit(solution)/shard_map/all_to_all | solution.py:109
  (22 shorter events, 0.3 us)
Async XLA Ops:
  0.6 37.0 %copy-start.1 = (bf16[128,1024]{1,0:T(8,128)(2,1)S(1)}, bf16[128,1024]{1,0:T(8,128)(2,1)}, u32[]{:S(2)}) copy-start(bf16[128,1024]{1,0:T(8,128)(2,1)} %param.9) | copy-start | bytes 786436
  0.6 36.9 %copy-start = (bf16[128,1024]{1,0:T(8,128)(2,1)S(1)}, bf16[128,1024]{1,0:T(8,128)(2,1)}, u32[]{:S(2)}) copy-start(bf16[128,1024]{1,0:T(8,128)(2,1)} %param.6) | copy-start | bytes 786436
  19.7 17.9 %collective-permute-start = (bf16[1,64,256]{2,1,0:T(8,128)(2,1)S(1)}, bf16[1,64,256]{2,1,0:T(8,128)(2,1)S(1)}, u32[]{:S(2)}, u32[]{:S(2)}) collective-permute-start(bf16[1,64,256]{2,1,0:T(8,128)(2,1)S(1)} %copy.111), channel_id=1, source_target_pairs={{0,4},{4,8},{8,12},{12,16},{16,20},{20,24},{24,28},{1,5},{5,9},{9,... | collective-permute-start | bytes 98312 | tf_op jit(solution)/shard_map/ppermute | solution.py:18
  24.7 13.0 %collective-permute-start.1 = (bf16[1,64,256]{2,1,0:T(8,128)(2,1)S(1)}, bf16[1,64,256]{2,1,0:T(8,128)(2,1)S(1)}, u32[]{:S(2)}, u32[]{:S(2)}) collective-permute-start(bf16[1,64,256]{2,1,0:T(8,128)(2,1)S(1)} %copy.112), channel_id=1, source_target_pairs={{0,8},{4,12},{8,16},{12,20},{16,24},{20,28},{1,9},{5,13},{9,17},{1... | collective-permute-start | bytes 98312 | tf_op jit(solution)/shard_map/ppermute | solution.py:18
  27.4 10.3 %collective-permute-start.2 = (bf16[1,64,256]{2,1,0:T(8,128)(2,1)S(1)}, bf16[1,64,256]{2,1,0:T(8,128)(2,1)S(1)}, u32[]{:S(2)}, u32[]{:S(2)}) collective-permute-start(bf16[1,64,256]{2,1,0:T(8,128)(2,1)S(1)} %copy.113), channel_id=1, source_target_pairs={{0,16},{4,20},{8,24},{12,28},{1,17},{5,21},{9,25},{13,29},{2,18},{... | collective-permute-start | bytes 98312 | tf_op jit(solution)/shard_map/ppermute | solution.py:18
  40.9 21.9 %copy-start.2 = (pred[2]{0:T(512)(128)(4,1)S(1)}, pred[2]{0:T(512)(128)(4,1)}, u32[]{:S(2)}) copy-start(pred[2]{0:T(512)(128)(4,1)} %constant.73.clone.1) | copy-start | bytes 10
  40.9 18.0 %collective-permute-start.5 = (bf16[1,64,256]{2,1,0:T(8,128)(2,1)S(1)}, bf16[1,64,256]{2,1,0:T(8,128)(2,1)S(1)}, u32[]{:S(2)}, u32[]{:S(2)}) collective-permute-start(bf16[1,64,256]{2,1,0:T(8,128)(2,1)S(1)} %get-tuple-element.21), channel_id=1, source_target_pairs={{16,0},{20,4},{24,8},{28,12},{17,1},{21,5},{25,9},{29,13},{18,2},{... | collective-permute-start | bytes 98312 | tf_op jit(solution)/shard_map/ppermute | solution.py:18
  48.6 15.0 %all-to-all-start = ((bf16[4,32,1024]{2,1,0:T(8,128)(2,1)}), bf16[4,32,1024]{2,1,0:T(8,128)(2,1)S(1)}, u32[]{:S(2)}, u32[]{:S(2)}) async-start(bf16[4,32,1024]{2,1,0:T(8,128)(2,1)} %all_to_all.14), calls=%async_computation | async-start | bytes 524288 | tf_op jit(solution)/shard_map/all_to_all | solution.py:109
  52.5 6.5 %collective-permute-start.4 = (bf16[1,64,256]{2,1,0:T(8,128)(2,1)S(1)}, bf16[1,64,256]{2,1,0:T(8,128)(2,1)S(1)}, u32[]{:S(2)}, u32[]{:S(2)}) collective-permute-start(bf16[1,64,256]{2,1,0:T(8,128)(2,1)S(1)} %get-tuple-element.22), channel_id=1, source_target_pairs={{8,0},{12,4},{16,8},{20,12},{24,16},{28,20},{9,1},{13,5},{17,9},{2... | collective-permute-start | bytes 98312 | tf_op jit(solution)/shard_map/ppermute | solution.py:18
  57.0 5.8 %collective-permute-start.3 = (bf16[1,64,256]{2,1,0:T(8,128)(2,1)S(1)}, bf16[1,64,256]{2,1,0:T(8,128)(2,1)S(1)}, u32[]{:S(2)}, u32[]{:S(2)}) collective-permute-start(bf16[1,64,256]{2,1,0:T(8,128)(2,1)S(1)} %get-tuple-element.20), channel_id=1, source_target_pairs={{4,0},{8,4},{12,8},{16,12},{20,16},{24,20},{28,24},{5,1},{9,5},{13... | collective-permute-start | bytes 98312 | tf_op jit(solution)/shard_map/ppermute | solution.py:18
where the time goes:
time: 64.9 us; the launch traced here: 64.3 us
  starting transfers between devices  21.9 us (34%)
  blocking collectives  16 us (25%)
  local copies, waits for them, and re-layouts  9.51 us (15%)
  other arithmetic  6.18 us (10%)
  waiting for transfers between devices  3.84 us (6%)
  between operations  3.63 us (6%)
  matrix products  3.32 us (5%)
    ppermute x6, starting transfers between devices, from_behind(): lax.ppermute(value, axis, [(source, source + steps) for source in range(i...  18 us
    all_gather x1, blocking collectives, on_device(): lax.all_gather(selected, 'ctx', axis=0, tiled=True)  16 us
    gather x2, other arithmetic, on_device(): key_pos = selected[:, slot_index] * KBLK + offsets  4.48 us
    all_to_all x1, starting transfers between devices, on_device(): lax.all_to_all(grad_flat, 'kvh', split_axis=0, concat_axis=1, tiled=True)  3.88 us
    ppermute x6, waiting for transfers between devices, from_behind(): lax.ppermute(value, axis, [(source, source + steps) for source in range(i...  3.84 us
    unnamed x14, local copies, waits for them, and re-layouts  1.8 us
    slice x3, local copies, waits for them, and re-layouts, on_device(): wanted_index = askers[section][:, section + 1] - own_index * key_blocks  1.75 us
    gather x1, local copies, waits for them, and re-layouts, on_device(): key_pos = selected[:, slot_index] * KBLK + offsets  1.62 us
  transfers between devices with their start and end apart: 7, of which 1 were waited for; matrix products, arithmetic and copies ran while one was open for 19% of the time, Pallas kernels for 0%

commit v1 on v0

v1 whole, which is shorter than its diff:
```python
import functools
import math

import jax
import jax.numpy as jnp
from jax import lax
from jax.experimental import pallas as pl
from jax.experimental.pallas import tpu as pltpu
from jax.sharding import PartitionSpec as P

HD = 128
GROUP = 8
KBLK = 64
QBLK = 128
SLOTS = 8
PAIR = 2

MESH = pl.DeviceIdType.MESH
LOG2E = math.log2(math.e)
NT = (((1,), (1,)), ((), ()))
NN = (((1,), (0,)), ((), ()))


def dot(a, b, dims):
    return lax.dot_general(a, b, dims, preferred_element_type=jnp.float32)


def kernel(
    ctx_count,
    kvh_count,
    distances,
    sel_ref,
    cnt_ref,
    q_hbm,
    k_hbm,
    v_hbm,
    u_hbm,
    att_hbm,
    gq_hbm,
    gk_hbm,
    gv_hbm,
    q_v,
    u_v,
    k_own,
    v_own,
    k_in,
    v_in,
    sel_out,
    sel_in,
    keys,
    vals,
    att_v,
    gq_v,
    terms,
    terms_out,
    terms_in,
    total,
    load_sem,
    store_sem,
    kv_send,
    kv_recv,
    sel_send,
    sel_recv,
    term_send,
    term_recv,
    gq_send,
    gq_recv,
    gq_local,
):
    score_scale = 1.0 / math.sqrt(HD)
    me = lax.axis_index("ctx")
    head = lax.axis_index("kvh")
    slots = 1 + len(distances)
    part = QBLK // kvh_count
    width = GROUP * HD
    chunks = GROUP // PAIR

    loads = [
        pltpu.make_async_copy(src, dst, load_sem.at[i])
        for i, (src, dst) in enumerate(
            [(k_hbm, k_own), (v_hbm, v_own), (q_hbm, q_v), (u_hbm, u_v)]
        )
    ]
    for copy in loads:
        copy.start()

    barrier = pltpu.get_barrier_semaphore()
    for r in range(1, kvh_count):
        peer = lax.rem(head + r, kvh_count)
        pl.semaphore_signal(barrier, inc=1, device_id={"kvh": peer}, device_id_type=MESH)
    for d in distances:

        @pl.when(me + d < ctx_count)
        def _():
            pl.semaphore_signal(barrier, inc=1, device_id={"ctx": me + d}, device_id_type=MESH)

        @pl.when(me - d >= 0)
        def _():
            pl.semaphore_signal(barrier, inc=1, device_id={"ctx": me - d}, device_id_type=MESH)

    for j, d in enumerate(distances):
        sel_out[j] = jnp.full((8, HD), sel_ref[0, j + 1] - 2 * (me - d), jnp.int32)

    partners = kvh_count - 1
    for d in distances:
        partners += 1 - (me + d) // ctx_count + (me - d + ctx_count) // ctx_count
    pl.semaphore_wait(barrier, partners)

    def remote(src, dst, send, recv, **where):
        return pltpu.make_async_remote_copy(
            src_ref=src, dst_ref=dst, send_sem=send, recv_sem=recv,
            device_id=where, device_id_type=MESH,
        )

    def k_copy(j, d):
        return remote(k_hbm, k_in.at[j], kv_send.at[0, j], kv_recv.at[0, j], ctx=me + d)

    def v_copy(j, d):
        return remote(v_hbm, v_in.at[j], kv_send.at[1, j], kv_recv.at[1, j], ctx=me + d)

    def sel_copy(j, d):
        return remote(sel_out.at[j], sel_in.at[j], sel_send.at[j], sel_recv.at[j], ctx=me - d)

    def term_copy(j, d):
        return remote(terms_out.at[j], terms_in.at[j], term_send.at[j], term_recv.at[j], ctx=me - d)

    def gq_copy(c, r):
        cols = PAIR * HD
        peer = lax.rem(head + r, kvh_count)
        return remote(
            gq_v.at[pl.ds(pl.multiple_of(peer * part, part), part), pl.ds(c * cols, cols)],
            gq_hbm.at[:, pl.ds(pl.multiple_of(head * width + c * cols, cols), cols)],
            gq_send.at[c, r - 1],
            gq_recv.at[c, r - 1],
            kvh=peer,
        )

    by_far = list(enumerate(distances))[::-1]
    for make in (k_copy, v_copy):
        for j, d in by_far:

            @pl.when(me + d < ctx_count)
            def _(make=make, j=j, d=d):
                make(j, d).start()

    for j, d in by_far:

        @pl.when(me - d >= 0)
        def _(j=j, d=d):
            sel_copy(j, d).start()

    for copy in loads:
        copy.wait()
    keys[0:KBLK] = k_own[0:KBLK]
    vals[0:KBLK] = v_own[0:KBLK]
    count = cnt_ref[0]
    for make, arrived, chosen in ((k_copy, k_in, keys), (v_copy, v_in, vals)):
        for j, d in enumerate(distances):

            @pl.when(me - d >= 0)
            def _(make=make, j=j, d=d):
                make(j, d).wait_recv()

            live = jnp.full((KBLK, HD), count > j + 1)
            upper = jnp.full((KBLK, HD), sel_ref[0, j + 1] - 2 * (me - d) > 0)
            lo = arrived[j, 0:KBLK].astype(jnp.float32)
            hi = arrived[j, KBLK : 2 * KBLK].astype(jnp.float32)
            rows = jnp.where(live, jnp.where(upper, hi, lo), 0.0)
            chosen[(j + 1) * KBLK : (j + 2) * KBLK] = rows.astype(jnp.bfloat16)

    k_all = keys[...]
    v_all = vals[...]
    k_t = k_all.astype(jnp.float32).T.astype(jnp.bfloat16)
    v_t = v_all.astype(jnp.float32).T.astype(jnp.bfloat16)

    lanes = PAIR * QBLK
    key_at = lax.broadcasted_iota(jnp.int32, (KBLK, lanes), 0)
    query_at = lax.rem(lax.broadcasted_iota(jnp.int32, (KBLK, lanes), 1), QBLK)
    causal = key_at <= query_at
    hidden = [jnp.full((KBLK, lanes), count <= j) for j in range(1, slots)]

    for c in range(chunks):
        heads = [slice((c * PAIR + i) * HD, (c * PAIR + i + 1) * HD) for i in range(PAIR)]
        q = jnp.concatenate([q_v[:, h] for h in heads], axis=0)
        u = jnp.concatenate([u_v[:, h] for h in heads], axis=0)
        s = dot(k_all, q, NT)
        s = jnp.concatenate(
            [jnp.where(causal, s[0:KBLK], -1e30)]
            + [
                jnp.where(hidden[j - 1], -1e30, s[j * KBLK : (j + 1) * KBLK])
                for j in range(1, slots)
            ],
            axis=0,
        )
        peak = jnp.max(s, axis=0, keepdims=True)
        e = jnp.exp2((s - peak) * (score_scale * LOG2E))
        p = e * (1.0 / jnp.sum(e, axis=0, keepdims=True))
        p_half = p.astype(jnp.bfloat16)
        dp = dot(v_all, u, NT)
        row_term = jnp.sum(p * dp, axis=0, keepdims=True)
        ds = (p * (dp - row_term)).astype(jnp.bfloat16)
        gq_t = dot(k_t, ds, NN) * score_scale
        att_t = dot(v_t, p_half, NN)
        for i, h in enumerate(heads):
            gq_v[:, h] = gq_t[:, i * QBLK : (i + 1) * QBLK].T.astype(jnp.bfloat16)
            att_v[:, h] = att_t[:, i * QBLK : (i + 1) * QBLK].T.astype(jnp.bfloat16)
        for r in range(1, kvh_count):
            gq_copy(c, r).start()
        k_term = dot(ds, q, NN) * score_scale
        v_term = dot(p_half, u, NN)
        if c == 0:
            terms[0] = k_term
            terms[1] = v_term
        else:
            terms[0] += k_term
            terms[1] += v_term

    for j, d in by_far:
        rows = slice((j + 1) * KBLK, (j + 2) * KBLK)
        terms_out[j, 0:KBLK] = terms[0, rows].astype(jnp.bfloat16)
        terms_out[j, KBLK : 2 * KBLK] = terms[1, rows].astype(jnp.bfloat16)

        @pl.when(me - d >= 0)
        def _(j=j, d=d):
            term_copy(j, d).start()

    att_store = pltpu.make_async_copy(att_v, att_hbm, store_sem.at[0])
    att_store.start()
    gq_store = pltpu.make_async_copy(
        gq_v.at[pl.ds(pl.multiple_of(head * part, part), part), :],
        gq_hbm.at[:, pl.ds(pl.multiple_of(head * width, width), width)],
        gq_local,
    )
    gq_store.start()

    for i in range(2):
        total[i, 0:KBLK] = terms[i, 0:KBLK]
        total[i, KBLK : 2 * KBLK] = jnp.zeros((KBLK, HD), jnp.float32)
    for j, d in enumerate(distances):

        @pl.when(me + d < ctx_count)
        def _(j=j, d=d):
            sel_copy(j, d).wait_recv()
            term_copy(j, d).wait_recv()
            where = jnp.broadcast_to(sel_in[j, 0:1], (KBLK, HD))
            for i in range(2):
                term = terms_in[j, i * KBLK : (i + 1) * KBLK].astype(jnp.float32)
                total[i, 0:KBLK] += jnp.where(where == 0, term, 0.0)
                total[i, KBLK : 2 * KBLK] += jnp.where(where == 1, term, 0.0)

    gk_store = pltpu.make_async_copy(total.at[0], gk_hbm, store_sem.at[1])
    gv_store = pltpu.make_async_copy(total.at[1], gv_hbm, store_sem.at[2])
    gk_store.start()
    gv_store.start()

    for j, d in enumerate(distances):

        @pl.when(me + d < ctx_count)
        def _(j=j, d=d):
            k_copy(j, d).wait_send()
            v_copy(j, d).wait_send()

        @pl.when(me - d >= 0)
        def _(j=j, d=d):
            sel_copy(j, d).wait_send()
            term_copy(j, d).wait_send()

    for c in range(chunks):
        for r in range(1, kvh_count):
            gq_copy(c, r).wait()
    gq_store.wait()
    att_store.wait()
    gk_store.wait()
    gv_store.wait()


def solution(mesh):
    ctx_count = mesh.shape["ctx"]
    kvh_count = mesh.shape["kvh"]
    distances = [1 << j for j in range(SLOTS - 1) if 1 << j < ctx_count]
    far = len(distances)
    slots = 1 + far

    def on_device(queries, keys, values, upstream, selected, counts):
        tokens, width = queries.shape
        key_rows = keys.shape[0]
        assert tokens == QBLK and key_rows == 2 * KBLK and selected.shape[0] == 1
        chunks = GROUP // PAIR
        bf16, f32 = jnp.bfloat16, jnp.float32
        dma = pltpu.SemaphoreType.DMA
        smem = pl.BlockSpec(memory_space=pltpu.SMEM)
        anywhere = pl.BlockSpec(memory_space=pl.ANY)
        return pl.pallas_call(
            functools.partial(kernel, ctx_count, kvh_count, distances),
            out_shape=(
                jax.ShapeDtypeStruct((tokens, width), bf16),
                jax.ShapeDtypeStruct((tokens // kvh_count, width * kvh_count), bf16),
                jax.ShapeDtypeStruct((key_rows, HD), f32),
                jax.ShapeDtypeStruct((key_rows, HD), f32),
            ),
            in_specs=[smem, smem] + [anywhere] * 4,
            out_specs=[anywhere] * 4,
            scratch_shapes=[
                pltpu.VMEM((tokens, width), bf16),
                pltpu.VMEM((tokens, width), bf16),
                pltpu.VMEM((key_rows, HD), bf16),
                pltpu.VMEM((key_rows, HD), bf16),
                pltpu.VMEM((far, key_rows, HD), bf16),
                pltpu.VMEM((far, key_rows, HD), bf16),
                pltpu.VMEM((far, 8, HD), jnp.int32),
                pltpu.VMEM((far, 8, HD), jnp.int32),
                pltpu.VMEM((slots * KBLK, HD), bf16),
                pltpu.VMEM((slots * KBLK, HD), bf16),
                pltpu.VMEM((tokens, width), bf16),
                pltpu.VMEM((tokens, width), bf16),
                pltpu.VMEM((2, slots * KBLK, HD), f32),
                pltpu.VMEM((far, 2 * KBLK, HD), bf16),
                pltpu.VMEM((far, 2 * KBLK, HD), bf16),
                pltpu.VMEM((2, key_rows, HD), f32),
                dma((4,)),
                dma((3,)),
                dma((2, far)),
                dma((2, far)),
                dma((far,)),
                dma((far,)),
                dma((far,)),
                dma((far,)),
                dma((chunks, kvh_count - 1)),
                dma((chunks, kvh_count - 1)),
                dma,
            ],
            compiler_params=pltpu.CompilerParams(
                collective_id=0, has_side_effects=True, vmem_limit_bytes=32 * 1024 * 1024
            ),
        )(selected, counts, queries, keys, values, upstream)

    placed = (
        P("ctx", "kvh"),
        P("ctx", "kvh"),
        P("ctx", "kvh"),
        P("ctx", "kvh"),
        P("ctx", None),
        P("ctx"),
    )
    return jax.shard_map(
        on_device,
        mesh=mesh,
        in_specs=placed,
        out_specs=(P("ctx", "kvh"), P(("ctx", "kvh"), None), P("ctx", "kvh"), P("ctx", "kvh")),
        check_vma=False,
    )
```

time: 64.9 us -> 27.6 us (0.43)
  the two profiles are of different devices: /device:TPU:28 before, /device:TPU:0 now
where the time goes in v1:
time: 27.6 us; the launch traced here: 27.3 us
  Pallas kernels  19.9 us (72%)
  local copies, waits for them, and re-layouts  6.08 us (22%)
  between operations  1.33 us (5%)
    pallas_call x1, Pallas kernels, on_device(): pl.pallas_call(functools.partial(kernel, ctx_count, kvh_count, distances)...  19.9 us
    unnamed x14, local copies, waits for them, and re-layouts  6.08 us

profile of v1, /device:TPU:0, one launch (start us, length us, event | category | flops | bytes accessed | tf_op | source)
XLA Modules:
  0.0 27.3 jit_solution(15489891818278273193)
XLA Ops:
  0.6 0.0 copy-start.4
  1.3 0.0 copy-done.4
  1.3 0.0 copy-start
  1.3 0.9 %copy-done = bf16[128,1024]{1,0:T(8,128)(2,1)S(1)} copy-done((bf16[128,1024]{1,0:T(8,128)(2,1)S(1)}, bf16[128,1024]{1,0:T(8,128)(2,1)}, u32[]{:S(2)}) %copy-start) | copy-done | bytes 262168
  2.3 0.0 copy-start.1
  2.3 0.9 %copy-done.1 = bf16[128,1024]{1,0:T(8,128)(2,1)S(1)} copy-done((bf16[128,1024]{1,0:T(8,128)(2,1)S(1)}, bf16[128,1024]{1,0:T(8,128)(2,1)}, u32[]{:S(2)}) %copy-start.1) | copy-done | bytes 262168
  3.2 0.0 copy-start.2
  3.2 0.8 %copy-done.2 = bf16[128,128]{1,0:T(8,128)(2,1)S(1)} copy-done((bf16[128,128]{1,0:T(8,128)(2,1)S(1)}, bf16[128,128]{1,0:T(8,128)(2,1)}, u32[]{:S(2)}) %copy-start.2) | copy-done | bytes 32792
  4.0 0.0 copy-start.3
  4.0 0.8 %copy-done.3 = bf16[128,128]{1,0:T(8,128)(2,1)S(1)} copy-done((bf16[128,128]{1,0:T(8,128)(2,1)S(1)}, bf16[128,128]{1,0:T(8,128)(2,1)}, u32[]{:S(2)}) %copy-start.3) | copy-done | bytes 32792
  4.7 19.9 %shard_map.93 = (bf16[128,1024]{1,0:T(8,128)(2,1)S(1)}, bf16[32,4096]{1,0:T(8,128)(2,1)S(1)}, f32[128,128]{1,0:T(8,128)S(1)}, f32[128,128]{1,0:T(8,128)S(1)}) custom-call(s32[1,8]{1,0:T(1,128)S(1)} %copy-done.4, s32[1]{0:T(128)S(6)} %copy.14.cnt_ref, bf16[128,1024]{1,0:T(8,128)(2,1)S(1)} %copy-done, bf16[128,128]{1,0:T(8,128)(2,1)S(1)} %copy-done.2, ...), custom_call_target="tpu_custom_call" | custom-call | tf_op jit(solution)/shard_map/pallas_call | solution.py:293
  24.6 0.7 %copy.15 = bf16[128,1024]{1,0:T(8,128)(2,1)} copy(bf16[128,1024]{1,0:T(8,128)(2,1)S(1)} %get-tuple-element.8) | data formatting | bytes 524288
  25.3 0.7 %copy.16 = bf16[32,4096]{1,0:T(8,128)(2,1)} copy(bf16[32,4096]{1,0:T(8,128)(2,1)S(1)} %get-tuple-element.9) | data formatting | bytes 524288
  26.0 0.6 %copy.17 = f32[128,128]{1,0:T(8,128)} copy(f32[128,128]{1,0:T(8,128)S(1)} %get-tuple-element.10) | data formatting | bytes 131072
  26.7 0.6 %copy.18 = f32[128,128]{1,0:T(8,128)} copy(f32[128,128]{1,0:T(8,128)S(1)} %get-tuple-element.11) | data formatting | bytes 131072
Async XLA Ops:
  0.6 0.7 %copy-start.4 = (s32[1,8]{1,0:T(1,128)S(1)}, s32[1,8]{1,0:T(1,128)}, u32[]{:S(2)}) copy-start(s32[1,8]{1,0:T(1,128)} %sel_ref.1) | copy-start | bytes 100
  1.3 1.0 %copy-start = (bf16[128,1024]{1,0:T(8,128)(2,1)S(1)}, bf16[128,1024]{1,0:T(8,128)(2,1)}, u32[]{:S(2)}) copy-start(bf16[128,1024]{1,0:T(8,128)(2,1)} %q_hbm.1) | copy-start | bytes 786436
  2.3 0.9 %copy-start.1 = (bf16[128,1024]{1,0:T(8,128)(2,1)S(1)}, bf16[128,1024]{1,0:T(8,128)(2,1)}, u32[]{:S(2)}) copy-start(bf16[128,1024]{1,0:T(8,128)(2,1)} %u_hbm.1) | copy-start | bytes 786436
  3.2 0.8 %copy-start.2 = (bf16[128,128]{1,0:T(8,128)(2,1)S(1)}, bf16[128,128]{1,0:T(8,128)(2,1)}, u32[]{:S(2)}) copy-start(bf16[128,128]{1,0:T(8,128)(2,1)} %k_hbm.1) | copy-start | bytes 98308
  4.0 0.8 %copy-start.3 = (bf16[128,128]{1,0:T(8,128)(2,1)S(1)}, bf16[128,128]{1,0:T(8,128)(2,1)}, u32[]{:S(2)}) copy-start(bf16[128,128]{1,0:T(8,128)(2,1)} %v_hbm.1) | copy-start | bytes 98308

commit v2 on v1

v2 whole, which is shorter than its diff:
```python
import functools
import math

import jax
import jax.numpy as jnp
from jax import lax
from jax.experimental import pallas as pl
from jax.experimental.pallas import tpu as pltpu
from jax.sharding import PartitionSpec as P

HD = 128
GROUP = 8
KBLK = 64
QBLK = 128
SLOTS = 8
PAIR = 2

MESH = pl.DeviceIdType.MESH
LOG2E = math.log2(math.e)
NN = (((1,), (0,)), ((), ()))


def dot(a, b, dims):
    return lax.dot_general(a, b, dims, preferred_element_type=jnp.float32)


def kernel(
    ctx_count,
    kvh_count,
    distances,
    cnt_ref,
    sel_hbm,
    q_hbm,
    k_hbm,
    v_hbm,
    u_hbm,
    att_out,
    gq_out,
    own_out,
    terms_in,
    sel_in,
    sel_ref,
    q_v,
    u_v,
    q_t,
    u_t,
    k_own,
    v_own,
    k_in,
    v_in,
    sel_out,
    keys,
    vals,
    prob,
    prob_half,
    grad_scores,
    att_v,
    gq_v,
    own,
    terms_out,
    load_sem,
    store_sem,
    kv_send,
    kv_recv,
    sel_send,
    sel_recv,
    term_send,
    term_recv,
    gq_send,
    gq_recv,
):
    score_scale = 1.0 / math.sqrt(HD)
    bf16, f32 = jnp.bfloat16, jnp.float32
    me = lax.axis_index("ctx")
    head = lax.axis_index("kvh")
    slots = 1 + len(distances)
    part = QBLK // kvh_count
    width = GROUP * HD
    chunks = GROUP // PAIR
    lanes = PAIR * QBLK

    loads = [
        pltpu.make_async_copy(src, dst, load_sem.at[i])
        for i, (src, dst) in enumerate(
            [
                (sel_hbm, sel_ref),
                (k_hbm, k_own),
                (v_hbm, v_own),
                (q_hbm, q_v),
                (u_hbm, u_v),
            ]
        )
    ]
    for copy in loads:
        copy.start()

    barrier = pltpu.get_barrier_semaphore()
    for r in range(1, kvh_count):
        peer = lax.rem(head + r, kvh_count)
        pl.semaphore_signal(barrier, inc=1, device_id={"kvh": peer}, device_id_type=MESH)
    for d in distances:

        @pl.when(me + d < ctx_count)
        def _():
            pl.semaphore_signal(barrier, inc=1, device_id={"ctx": me + d}, device_id_type=MESH)

        @pl.when(me - d >= 0)
        def _():
            pl.semaphore_signal(barrier, inc=1, device_id={"ctx": me - d}, device_id_type=MESH)

    for copy in loads[:3]:
        copy.wait()
    for j, d in enumerate(distances):
        sel_out[j] = jnp.full((8, HD), sel_ref[0, j + 1] - 2 * (me - d), jnp.int32)

    partners = kvh_count - 1
    for d in distances:
        partners += 1 - (me + d) // ctx_count + (me - d + ctx_count) // ctx_count
    pl.semaphore_wait(barrier, partners)

    def remote(src, dst, send, recv, **where):
        return pltpu.make_async_remote_copy(
            src_ref=src, dst_ref=dst, send_sem=send, recv_sem=recv,
            device_id=where, device_id_type=MESH,
        )

    def k_copy(j, d):
        return remote(k_own, k_in.at[j], kv_send.at[0, j], kv_recv.at[0, j], ctx=me + d)

    def v_copy(j, d):
        return remote(v_own, v_in.at[j], kv_send.at[1, j], kv_recv.at[1, j], ctx=me + d)

    def sel_copy(j, d):
        return remote(sel_out.at[j], sel_in.at[j], sel_send.at[j], sel_recv.at[j], ctx=me - d)

    def term_copy(i, j, d):
        return remote(
            terms_out.at[i, j], terms_in.at[i, j], term_send.at[i, j], term_recv.at[i, j], ctx=me - d
        )

    def gq_copy(c, r):
        cols = PAIR * HD
        peer = lax.rem(head + r, kvh_count)
        return remote(
            gq_v.at[pl.ds(pl.multiple_of(peer * part, part), part), pl.ds(c * cols, cols)],
            gq_out.at[:, pl.ds(pl.multiple_of(head * width + c * cols, cols), cols)],
            gq_send.at[c, r - 1],
            gq_recv.at[c, r - 1],
            kvh=peer,
        )

    by_far = list(enumerate(distances))[::-1]
    for make in (k_copy, v_copy):
        for j, d in by_far:

            @pl.when(me + d < ctx_count)
            def _(make=make, j=j, d=d):
                make(j, d).start()

    for j, d in by_far:

        @pl.when(me - d >= 0)
        def _(j=j, d=d):
            sel_copy(j, d).start()

    for copy in loads[3:]:
        copy.wait()
    for h in range(GROUP):
        at = slice(h * HD, (h + 1) * HD)
        q_t[:, at] = q_v[:, at].astype(f32).T.astype(bf16)
        u_t[:, at] = u_v[:, at].astype(f32).T.astype(bf16)

    count = cnt_ref[0]

    def receive(make, own_rows, arrived, chosen):
        chosen[0:KBLK] = own_rows[0:KBLK]
        for j, d in enumerate(distances):

            @pl.when(me - d >= 0)
            def _(j=j, d=d):
                make(j, d).wait_recv()

            live = jnp.full((KBLK, HD), count > j + 1)
            upper = jnp.full((KBLK, HD), sel_ref[0, j + 1] - 2 * (me - d) > 0)
            lo = arrived[j, 0:KBLK].astype(f32)
            hi = arrived[j, KBLK : 2 * KBLK].astype(f32)
            rows = jnp.where(live, jnp.where(upper, hi, lo), 0.0)
            chosen[(j + 1) * KBLK : (j + 2) * KBLK] = rows.astype(bf16)
        return chosen[...]

    def send_terms(i, term):
        own[i] = term[0:KBLK]
        for j, d in by_far:
            terms_out[i, j] = term[(j + 1) * KBLK : (j + 2) * KBLK].astype(bf16)

            @pl.when(me - d >= 0)
            def _(j=j, d=d):
                term_copy(i, j, d).start()

    def by_rows(ref):
        return jnp.concatenate([ref[:, h * HD : (h + 1) * HD] for h in range(GROUP)], axis=0)

    k_all = receive(k_copy, k_own, k_in, keys)
    key_at = lax.broadcasted_iota(jnp.int32, (KBLK, lanes), 0)
    query_at = lax.rem(lax.broadcasted_iota(jnp.int32, (KBLK, lanes), 1), QBLK)
    causal = key_at <= query_at
    hidden = [jnp.full((KBLK, lanes), count <= j) for j in range(1, slots)]
    for c in range(chunks):
        at = slice(c * lanes, (c + 1) * lanes)
        s = dot(k_all, q_t[:, at], NN)
        s = jnp.concatenate(
            [jnp.where(causal, s[0:KBLK], -1e30)]
            + [
                jnp.where(hidden[j - 1], -1e30, s[j * KBLK : (j + 1) * KBLK])
                for j in range(1, slots)
            ],
            axis=0,
        )
        peak = jnp.max(s, axis=0, keepdims=True)
        e = jnp.exp2((s - peak) * (score_scale * LOG2E))
        p = e * (1.0 / jnp.sum(e, axis=0, keepdims=True))
        prob[:, at] = p
        prob_half[:, at] = p.astype(bf16)
    send_terms(1, dot(prob_half[...], by_rows(u_v), NN))

    v_all = receive(v_copy, v_own, v_in, vals)
    k_t = k_all.astype(f32).T.astype(bf16)
    for c in range(chunks):
        at = slice(c * lanes, (c + 1) * lanes)
        dp = dot(v_all, u_t[:, at], NN)
        p = prob[:, at]
        row_term = jnp.sum(p * dp, axis=0, keepdims=True)
        ds = (p * (dp - row_term)).astype(bf16)
        grad_scores[:, at] = ds
        gq_c = dot(k_t, ds, NN) * score_scale
        for i in range(PAIR):
            h = c * PAIR + i
            gq_v[:, h * HD : (h + 1) * HD] = gq_c[:, i * QBLK : (i + 1) * QBLK].T.astype(bf16)
        for r in range(1, kvh_count):
            gq_copy(c, r).start()
    send_terms(0, dot(grad_scores[...], by_rows(q_v), NN) * score_scale)

    v_t = v_all.astype(f32).T.astype(bf16)
    for c in range(chunks):
        at = slice(c * lanes, (c + 1) * lanes)
        att_c = dot(v_t, prob_half[:, at], NN)
        for i in range(PAIR):
            h = c * PAIR + i
            att_v[:, h * HD : (h + 1) * HD] = att_c[:, i * QBLK : (i + 1) * QBLK].T.astype(bf16)

    stores = [
        pltpu.make_async_copy(
            gq_v.at[pl.ds(pl.multiple_of(head * part, part), part), :],
            gq_out.at[:, pl.ds(pl.multiple_of(head * width, width), width)],
            store_sem.at[0],
        ),
        pltpu.make_async_copy(own, own_out, store_sem.at[1]),
        pltpu.make_async_copy(att_v, att_out, store_sem.at[2]),
    ]
    for copy in stores:
        copy.start()

    for j, d in enumerate(distances):

        @pl.when(me + d < ctx_count)
        def _(j=j, d=d):
            k_copy(j, d).wait_send()
            v_copy(j, d).wait_send()
            sel_copy(j, d).wait_recv()
            term_copy(1, j, d).wait_recv()
            term_copy(0, j, d).wait_recv()

        @pl.when(me - d >= 0)
        def _(j=j, d=d):
            sel_copy(j, d).wait_send()
            term_copy(1, j, d).wait_send()
            term_copy(0, j, d).wait_send()

    for c in range(chunks):
        for r in range(1, kvh_count):
            gq_copy(c, r).wait()
    for copy in stores:
        copy.wait()


def finish(ctx_count, distances, att, gq, own, terms, sel, att_hbm, gq_hbm, gk_hbm, gv_hbm, total, sem):
    me = lax.axis_index("ctx")
    stores = [
        pltpu.make_async_copy(src, dst, sem.at[i])
        for i, (src, dst) in enumerate(
            [(att, att_hbm), (gq, gq_hbm), (total.at[0], gk_hbm), (total.at[1], gv_hbm)]
        )
    ]
    stores[0].start()
    stores[1].start()
    for i in range(2):
        total[i, 0:KBLK] = own[i]
        total[i, KBLK : 2 * KBLK] = jnp.zeros((KBLK, HD), jnp.float32)
    for j, d in enumerate(distances):

        @pl.when(me + d < ctx_count)
        def _(j=j, d=d):
            where = jnp.broadcast_to(sel[j, 0:1], (KBLK, HD))
            for i in range(2):
                term = terms[i, j].astype(jnp.float32)
                total[i, 0:KBLK] += jnp.where(where == 0, term, 0.0)
                total[i, KBLK : 2 * KBLK] += jnp.where(where == 1, term, 0.0)

    stores[2].start()
    stores[3].start()
    for copy in stores:
        copy.wait()


def solution(mesh):
    ctx_count = mesh.shape["ctx"]
    kvh_count = mesh.shape["kvh"]
    distances = [1 << j for j in range(SLOTS - 1) if 1 << j < ctx_count]
    far = len(distances)
    slots = 1 + far

    def on_device(queries, keys, values, upstream, selected, counts):
        tokens, width = queries.shape
        key_rows = keys.shape[0]
        assert tokens == QBLK and key_rows == 2 * KBLK and selected.shape[0] == 1
        chunks = GROUP // PAIR
        bf16, f32 = jnp.bfloat16, jnp.float32
        dma = pltpu.SemaphoreType.DMA
        smem = pl.BlockSpec(memory_space=pltpu.SMEM)
        hbm = pl.BlockSpec(memory_space=pltpu.HBM)
        vmem = pl.BlockSpec(memory_space=pltpu.VMEM)
        anywhere = pl.BlockSpec(memory_space=pl.ANY)
        result = [
            jax.ShapeDtypeStruct((tokens, width), bf16),
            jax.ShapeDtypeStruct((tokens // kvh_count, width * kvh_count), bf16),
        ]
        grad = jax.ShapeDtypeStruct((key_rows, HD), f32)
        parts = pl.pallas_call(
            functools.partial(kernel, ctx_count, kvh_count, distances),
            out_shape=result
            + [
                jax.ShapeDtypeStruct((2, KBLK, HD), f32),
                jax.ShapeDtypeStruct((2, far, KBLK, HD), bf16),
                jax.ShapeDtypeStruct((far, 8, HD), jnp.int32),
            ],
            in_specs=[smem] + [hbm] * 5,
            out_specs=[anywhere] * 5,
            scratch_shapes=[
                pltpu.SMEM((1, SLOTS), jnp.int32),
                pltpu.VMEM((tokens, width), bf16),
                pltpu.VMEM((tokens, width), bf16),
                pltpu.VMEM((HD, GROUP * tokens), bf16),
                pltpu.VMEM((HD, GROUP * tokens), bf16),
                pltpu.VMEM((key_rows, HD), bf16),
                pltpu.VMEM((key_rows, HD), bf16),
                pltpu.VMEM((far, key_rows, HD), bf16),
                pltpu.VMEM((far, key_rows, HD), bf16),
                pltpu.VMEM((far, 8, HD), jnp.int32),
                pltpu.VMEM((slots * KBLK, HD), bf16),
                pltpu.VMEM((slots * KBLK, HD), bf16),
                pltpu.VMEM((slots * KBLK, GROUP * tokens), f32),
                pltpu.VMEM((slots * KBLK, GROUP * tokens), bf16),
                pltpu.VMEM((slots * KBLK, GROUP * tokens), bf16),
                pltpu.VMEM((tokens, width), bf16),
                pltpu.VMEM((tokens, width), bf16),
                pltpu.VMEM((2, KBLK, HD), f32),
                pltpu.VMEM((2, far, KBLK, HD), bf16),
                dma((5,)),
                dma((3,)),
                dma((2, far)),
                dma((2, far)),
                dma((far,)),
                dma((far,)),
                dma((2, far)),
                dma((2, far)),
                dma((chunks, kvh_count - 1)),
                dma((chunks, kvh_count - 1)),
            ],
            compiler_params=pltpu.CompilerParams(
                collective_id=0, has_side_effects=True, vmem_limit_bytes=32 * 1024 * 1024
            ),
        )(
            counts,
            *[
                pltpu.with_memory_space_constraint(x, pltpu.HBM)
                for x in (selected, queries, keys, values, upstream)
            ],
        )
        return pl.pallas_call(
            functools.partial(finish, ctx_count, distances),
            out_shape=result + [grad, grad],
            in_specs=[anywhere, anywhere, vmem, vmem, vmem],
            out_specs=[hbm] * 4,
            scratch_shapes=[pltpu.VMEM((2, key_rows, HD), f32), dma((4,))],
        )(*parts)

    placed = (
        P("ctx", "kvh"),
        P("ctx", "kvh"),
        P("ctx", "kvh"),
        P("ctx", "kvh"),
        P("ctx", None),
        P("ctx"),
    )
    return jax.shard_map(
        on_device,
        mesh=mesh,
        in_specs=placed,
        out_specs=(P("ctx", "kvh"), P(("ctx", "kvh"), None), P("ctx", "kvh"), P("ctx", "kvh")),
        check_vma=False,
    )
```

time: 27.6 us -> 41.2 us (1.49)
  Pallas kernels: 19.9 us -> 36.5 us
  local copies, waits for them, and re-layouts: 6.08 us -> 3.23 us
    pallas_call x0 -> x1, Pallas kernels: none -> 17.9 us  [on_device(): pl.pallas_call(functools.partial(finish, ctx_count, distances), out_shape...]
    unnamed x14 -> x10, local copies, waits for them, and re-layouts: 6.08 us -> 3.23 us
    pallas_call x1, Pallas kernels: 19.9 us -> 18.6 us  [on_device(): pl.pallas_call(functools.partial(kernel, ctx_count, kvh_count, distances)...]
where the time goes in v2:
time: 41.2 us; the launch traced here: 41 us
  Pallas kernels  36.5 us (89%)
  local copies, waits for them, and re-layouts  3.23 us (8%)
  between operations  1.3 us (3%)
    pallas_call x1, Pallas kernels, on_device(): pl.pallas_call(functools.partial(kernel, ctx_count, kvh_count, distances)...  18.6 us
    pallas_call x1, Pallas kernels, on_device(): pl.pallas_call(functools.partial(finish, ctx_count, distances), out_shape...  17.9 us
    unnamed x10, local copies, waits for them, and re-layouts  3.23 us

profile of v2, /device:TPU:0, one launch (start us, length us, event | category | flops | bytes accessed | tf_op | source)
XLA Modules:
  0.0 41.0 jit_solution(10532849916918925227)
XLA Ops:
  1.3 18.6 %shard_map.93 = (bf16[128,1024]{1,0:T(8,128)(2,1)S(1)}, bf16[32,4096]{1,0:T(8,128)(2,1)S(1)}, f32[2,64,128]{2,1,0:T(8,128)S(1)}, bf16[2,3,64,128]{3,2,1,0:T(8,128)(2,1)S(1)}, s32[3,8,128]{2,1,0:T(8,128)S(1)}) custom-call(s32[1]{0:T(128)S(6)} %copy.10.cnt_ref, s32[1,8]{1,0:T(1,128)} %sel_hbm.1, bf16[128,1024]{1,0:T(8,128)(2,1)} %q_hbm.1, ...), custom_call_target="tpu_custom_call" | custom-call | tf_op jit(solution)/shard_map/pallas_call | solution.py:338
  19.9 0.0 copy-start
  19.9 0.7 %copy-done = bf16[128,1024]{1,0:T(8,128)(2,1)} copy-done((bf16[128,1024]{1,0:T(8,128)(2,1)}, bf16[128,1024]{1,0:T(8,128)(2,1)S(1)}, u32[]{:S(2)}) %copy-start) | copy-done | bytes 262168
  20.6 0.0 copy-start.1
  20.6 0.7 %copy-done.1 = bf16[32,4096]{1,0:T(8,128)(2,1)} copy-done((bf16[32,4096]{1,0:T(8,128)(2,1)}, bf16[32,4096]{1,0:T(8,128)(2,1)S(1)}, u32[]{:S(2)}) %copy-start.1) | copy-done | bytes 262168
  21.3 0.0 copy-start.2
  21.3 0.6 %copy-done.2 = bf16[2,3,64,128]{3,2,1,0:T(8,128)(2,1)} copy-done((bf16[2,3,64,128]{3,2,1,0:T(8,128)(2,1)}, bf16[2,3,64,128]{3,2,1,0:T(8,128)(2,1)S(1)}, u32[]{:S(2)}) %copy-start.2) | copy-done | bytes 98328
  21.9 0.0 copy-start.3
  21.9 0.6 %copy-done.3 = f32[2,64,128]{2,1,0:T(8,128)} copy-done((f32[2,64,128]{2,1,0:T(8,128)}, f32[2,64,128]{2,1,0:T(8,128)S(1)}, u32[]{:S(2)}) %copy-start.3) | copy-done | bytes 65560
  22.5 0.0 copy-start.4
  22.5 0.6 %copy-done.4 = s32[3,8,128]{2,1,0:T(8,128)} copy-done((s32[3,8,128]{2,1,0:T(8,128)}, s32[3,8,128]{2,1,0:T(8,128)S(1)}, u32[]{:S(2)}) %copy-start.4) | copy-done | bytes 12312
  23.1 17.9 %shard_map.94 = (bf16[128,1024]{1,0:T(8,128)(2,1)}, bf16[32,4096]{1,0:T(8,128)(2,1)}, f32[128,128]{1,0:T(8,128)}, f32[128,128]{1,0:T(8,128)}) custom-call(bf16[128,1024]{1,0:T(8,128)(2,1)} %copy-done, bf16[32,4096]{1,0:T(8,128)(2,1)} %copy-done.1, f32[2,64,128]{2,1,0:T(8,128)} %copy-done.3, bf16[2,3,64,128]{3,2,1,0:T(8,128)(2,1)} %copy-done.2, ...), custom_call_target="tpu_custom_call" | custom-call | tf_op jit(solution)/shard_map/pallas_call | solution.py:389
Async XLA Ops:
  19.9 0.7 %copy-start = (bf16[128,1024]{1,0:T(8,128)(2,1)}, bf16[128,1024]{1,0:T(8,128)(2,1)S(1)}, u32[]{:S(2)}) copy-start(bf16[128,1024]{1,0:T(8,128)(2,1)S(1)} %get-tuple-element.9.att) | copy-start | bytes 786436
  20.6 0.7 %copy-start.1 = (bf16[32,4096]{1,0:T(8,128)(2,1)}, bf16[32,4096]{1,0:T(8,128)(2,1)S(1)}, u32[]{:S(2)}) copy-start(bf16[32,4096]{1,0:T(8,128)(2,1)S(1)} %get-tuple-element.10.gq) | copy-start | bytes 786436
  21.3 0.6 %copy-start.2 = (bf16[2,3,64,128]{3,2,1,0:T(8,128)(2,1)}, bf16[2,3,64,128]{3,2,1,0:T(8,128)(2,1)S(1)}, u32[]{:S(2)}) copy-start(bf16[2,3,64,128]{3,2,1,0:T(8,128)(2,1)S(1)} %get-tuple-element.12.terms) | copy-start | bytes 294916
  21.9 0.6 %copy-start.3 = (f32[2,64,128]{2,1,0:T(8,128)}, f32[2,64,128]{2,1,0:T(8,128)S(1)}, u32[]{:S(2)}) copy-start(f32[2,64,128]{2,1,0:T(8,128)S(1)} %get-tuple-element.11.own) | copy-start | bytes 196612
  22.5 0.6 %copy-start.4 = (s32[3,8,128]{2,1,0:T(8,128)}, s32[3,8,128]{2,1,0:T(8,128)S(1)}, u32[]{:S(2)}) copy-start(s32[3,8,128]{2,1,0:T(8,128)S(1)} %get-tuple-element.13.sel) | copy-start | bytes 36868

commit v3 on v2

--- a/solution.py
+++ b/solution.py
@@ -38,7 +38,7 @@
     gq_out,
     own_out,
     terms_in,
-    sel_in,
+    sel_store,
     sel_ref,
     q_v,
     u_v,
@@ -46,9 +46,12 @@
     u_t,
     k_own,
     v_own,
+    k_out,
+    v_out,
     k_in,
     v_in,
     sel_out,
+    sel_in,
     keys,
     vals,
     prob,
@@ -125,10 +128,10 @@
         )
 
     def k_copy(j, d):
-        return remote(k_own, k_in.at[j], kv_send.at[0, j], kv_recv.at[0, j], ctx=me + d)
+        return remote(k_out.at[j], k_in.at[j], kv_send.at[0, j], kv_recv.at[0, j], ctx=me + d)
 
     def v_copy(j, d):
-        return remote(v_own, v_in.at[j], kv_send.at[1, j], kv_recv.at[1, j], ctx=me + d)
+        return remote(v_out.at[j], v_in.at[j], kv_send.at[1, j], kv_recv.at[1, j], ctx=me + d)
 
     def sel_copy(j, d):
         return remote(sel_out.at[j], sel_in.at[j], sel_send.at[j], sel_recv.at[j], ctx=me - d)
@@ -150,13 +153,6 @@
         )
 
     by_far = list(enumerate(distances))[::-1]
-    for make in (k_copy, v_copy):
-        for j, d in by_far:
-
-            @pl.when(me + d < ctx_count)
-            def _(make=make, j=j, d=d):
-                make(j, d).start()
-
     for j, d in by_far:
 
         @pl.when(me - d >= 0)
@@ -165,10 +161,29 @@
 
     for copy in loads[3:]:
         copy.wait()
-    for h in range(GROUP):
-        at = slice(h * HD, (h + 1) * HD)
-        q_t[:, at] = q_v[:, at].astype(f32).T.astype(bf16)
-        u_t[:, at] = u_v[:, at].astype(f32).T.astype(bf16)
+
+    def transpose(rows, columns):
+        for h in range(GROUP):
+            at = slice(h * HD, (h + 1) * HD)
+            columns[:, at] = rows[:, at].astype(f32).T.astype(bf16)
+
+    def send_rows(make, own_rows, out, first):
+        for j, d in enumerate(distances):
+
+            @pl.when(me + d < ctx_count)
+            def _(j=j, d=d):
+                if first:
+                    sel_copy(j, d).wait_recv()
+                upper = jnp.broadcast_to(sel_in[j, 0:1], (KBLK, HD)) > 0
+                lo = own_rows[0:KBLK].astype(f32)
+                hi = own_rows[KBLK : 2 * KBLK].astype(f32)
+                out[j] = jnp.where(upper, hi, lo).astype(bf16)
+                make(j, d).start()
+
+    transpose(q_v, q_t)
+    send_rows(k_copy, k_own, k_out, True)
+    send_rows(v_copy, v_own, v_out, False)
+    transpose(u_v, u_t)
 
     count = cnt_ref[0]
 
@@ -181,10 +196,7 @@
                 make(j, d).wait_recv()
 
             live = jnp.full((KBLK, HD), count > j + 1)
-            upper = jnp.full((KBLK, HD), sel_ref[0, j + 1] - 2 * (me - d) > 0)
-            lo = arrived[j, 0:KBLK].astype(f32)
-            hi = arrived[j, KBLK : 2 * KBLK].astype(f32)
-            rows = jnp.where(live, jnp.where(upper, hi, lo), 0.0)
+            rows = jnp.where(live, arrived[j].astype(f32), 0.0)
             chosen[(j + 1) * KBLK : (j + 2) * KBLK] = rows.astype(bf16)
         return chosen[...]
 
@@ -256,6 +268,7 @@
         ),
         pltpu.make_async_copy(own, own_out, store_sem.at[1]),
         pltpu.make_async_copy(att_v, att_out, store_sem.at[2]),
+        pltpu.make_async_copy(sel_in, sel_store, store_sem.at[3]),
     ]
     for copy in stores:
         copy.start()
@@ -266,7 +279,6 @@
         def _(j=j, d=d):
             k_copy(j, d).wait_send()
             v_copy(j, d).wait_send()
-            sel_copy(j, d).wait_recv()
             term_copy(1, j, d).wait_recv()
             term_copy(0, j, d).wait_recv()
 
@@ -353,8 +365,11 @@
                 pltpu.VMEM((HD, GROUP * tokens), bf16),
                 pltpu.VMEM((key_rows, HD), bf16),
                 pltpu.VMEM((key_rows, HD), bf16),
-                pltpu.VMEM((far, key_rows, HD), bf16),
-                pltpu.VMEM((far, key_rows, HD), bf16),
+                pltpu.VMEM((far, KBLK, HD), bf16),
+                pltpu.VMEM((far, KBLK, HD), bf16),
+                pltpu.VMEM((far, KBLK, HD), bf16),
+                pltpu.VMEM((far, KBLK, HD), bf16),
+                pltpu.VMEM((far, 8, HD), jnp.int32),
                 pltpu.VMEM((far, 8, HD), jnp.int32),
                 pltpu.VMEM((slots * KBLK, HD), bf16),
                 pltpu.VMEM((slots * KBLK, HD), bf16),
@@ -366,7 +381,7 @@
                 pltpu.VMEM((2, KBLK, HD), f32),
                 pltpu.VMEM((2, far, KBLK, HD), bf16),
                 dma((5,)),
-                dma((3,)),
+                dma((4,)),
                 dma((2, far)),
                 dma((2, far)),
                 dma((far,)),
@@ -392,6 +407,7 @@
             in_specs=[anywhere, anywhere, vmem, vmem, vmem],
             out_specs=[hbm] * 4,
             scratch_shapes=[pltpu.VMEM((2, key_rows, HD), f32), dma((4,))],
+            compiler_params=pltpu.CompilerParams(vmem_limit_bytes=4 * 1024 * 1024),
         )(*parts)
 
     placed = (

time: 41.2 us -> 20.2 us (0.49)
  Pallas kernels: 36.5 us -> 18.7 us
  local copies, waits for them, and re-layouts: 3.23 us -> 0 us
    pallas_call x1, Pallas kernels: 17.9 us -> 0.86 us  [on_device(): pl.pallas_call(functools.partial(finish, ctx_count, distances), out_shape...]
    unnamed x10 -> x0, local copies, waits for them, and re-layouts: 3.23 us -> none
    pallas_call x1, Pallas kernels: 18.6 us -> 17.8 us  [on_device(): pl.pallas_call(functools.partial(kernel, ctx_count, kvh_count, distances)...]
where the time goes in v3:
time: 20.2 us; the launch traced here: 20 us
  Pallas kernels  18.7 us (93%)
  between operations  1.29 us (6%)
    pallas_call x1, Pallas kernels, on_device(): pl.pallas_call(functools.partial(kernel, ctx_count, kvh_count, distances)...  17.8 us
    pallas_call x1, Pallas kernels, on_device(): pl.pallas_call(functools.partial(finish, ctx_count, distances), out_shape...  0.86 us

profile of v3, /device:TPU:0, one launch (start us, length us, event | category | flops | bytes accessed | tf_op | source)
XLA Modules:
  0.0 20.0 jit_solution(14668160651204975491)
XLA Ops:
  1.3 17.8 %shard_map.93 = (bf16[128,1024]{1,0:T(8,128)(2,1)S(1)}, bf16[32,4096]{1,0:T(8,128)(2,1)S(1)}, f32[2,64,128]{2,1,0:T(8,128)S(1)}, bf16[2,3,64,128]{3,2,1,0:T(8,128)(2,1)S(1)}, s32[3,8,128]{2,1,0:T(8,128)S(1)}) custom-call(s32[1]{0:T(128)S(6)} %copy.10.cnt_ref, s32[1,8]{1,0:T(1,128)} %sel_hbm.1, bf16[128,1024]{1,0:T(8,128)(2,1)} %q_hbm.1, ...), custom_call_target="tpu_custom_call" | custom-call | tf_op jit(solution)/shard_map/pallas_call | solution.py:350
  19.1 0.9 %shard_map.94 = (bf16[128,1024]{1,0:T(8,128)(2,1)}, bf16[32,4096]{1,0:T(8,128)(2,1)}, f32[128,128]{1,0:T(8,128)}, f32[128,128]{1,0:T(8,128)}) custom-call(bf16[128,1024]{1,0:T(8,128)(2,1)S(1)} %get-tuple-element.9.att, bf16[32,4096]{1,0:T(8,128)(2,1)S(1)} %get-tuple-element.10.gq, f32[2,64,128]{2,1,0:T(8,128)S(1)} %get-tuple-element.11.own, ...), custom_call_target="tpu_custom_call" | custom-call | tf_op jit(solution)/shard_map/pallas_call | solution.py:404

commit v4 on v3

--- a/solution.py
+++ b/solution.py
@@ -236,7 +236,6 @@
     send_terms(1, dot(prob_half[...], by_rows(u_v), NN))
 
     v_all = receive(v_copy, v_own, v_in, vals)
-    k_t = k_all.astype(f32).T.astype(bf16)
     for c in range(chunks):
         at = slice(c * lanes, (c + 1) * lanes)
         dp = dot(v_all, u_t[:, at], NN)
@@ -244,13 +243,17 @@
         row_term = jnp.sum(p * dp, axis=0, keepdims=True)
         ds = (p * (dp - row_term)).astype(bf16)
         grad_scores[:, at] = ds
-        gq_c = dot(k_t, ds, NN) * score_scale
+    send_terms(0, dot(grad_scores[...], by_rows(q_v), NN) * score_scale)
+
+    k_t = k_all.astype(f32).T.astype(bf16)
+    for c in range(chunks):
+        at = slice(c * lanes, (c + 1) * lanes)
+        gq_c = dot(k_t, grad_scores[:, at], NN) * score_scale
         for i in range(PAIR):
             h = c * PAIR + i
             gq_v[:, h * HD : (h + 1) * HD] = gq_c[:, i * QBLK : (i + 1) * QBLK].T.astype(bf16)
         for r in range(1, kvh_count):
             gq_copy(c, r).start()
-    send_terms(0, dot(grad_scores[...], by_rows(q_v), NN) * score_scale)
 
     v_t = v_all.astype(f32).T.astype(bf16)
     for c in range(chunks):

time: 20.2 us -> 18.6 us (0.921)
  Pallas kernels: 18.7 us -> 17.2 us
    pallas_call x1, Pallas kernels: 17.8 us -> 16.3 us  [on_device(): pl.pallas_call(functools.partial(kernel, ctx_count, kvh_count, distances)...]
where the time goes in v4:
time: 18.6 us; the launch traced here: 18.5 us
  Pallas kernels  17.2 us (92%)
  between operations  1.29 us (7%)
    pallas_call x1, Pallas kernels, on_device(): pl.pallas_call(functools.partial(kernel, ctx_count, kvh_count, distances)...  16.3 us
    pallas_call x1, Pallas kernels, on_device(): pl.pallas_call(functools.partial(finish, ctx_count, distances), out_shape...  0.86 us

profile of v4, /device:TPU:0, one launch (start us, length us, event | category | flops | bytes accessed | tf_op | source)
XLA Modules:
  0.0 18.5 jit_solution(2973670898476566404)
XLA Ops:
  1.3 16.3 %shard_map.93 = (bf16[128,1024]{1,0:T(8,128)(2,1)S(1)}, bf16[32,4096]{1,0:T(8,128)(2,1)S(1)}, f32[2,64,128]{2,1,0:T(8,128)S(1)}, bf16[2,3,64,128]{3,2,1,0:T(8,128)(2,1)S(1)}, s32[3,8,128]{2,1,0:T(8,128)S(1)}) custom-call(s32[1]{0:T(128)S(6)} %copy.10.cnt_ref, s32[1,8]{1,0:T(1,128)} %sel_hbm.1, bf16[128,1024]{1,0:T(8,128)(2,1)} %q_hbm.1, ...), custom_call_target="tpu_custom_call" | custom-call | tf_op jit(solution)/shard_map/pallas_call | solution.py:353
  17.6 0.9 %shard_map.94 = (bf16[128,1024]{1,0:T(8,128)(2,1)}, bf16[32,4096]{1,0:T(8,128)(2,1)}, f32[128,128]{1,0:T(8,128)}, f32[128,128]{1,0:T(8,128)}) custom-call(bf16[128,1024]{1,0:T(8,128)(2,1)S(1)} %get-tuple-element.9.att, bf16[32,4096]{1,0:T(8,128)(2,1)S(1)} %get-tuple-element.10.gq, f32[2,64,128]{2,1,0:T(8,128)S(1)} %get-tuple-element.11.own, ...), custom_call_target="tpu_custom_call" | custom-call | tf_op jit(solution)/shard_map/pallas_call | solution.py:407

commit v5 on v4

--- a/solution.py
+++ b/solution.py
@@ -145,7 +145,7 @@
         cols = PAIR * HD
         peer = lax.rem(head + r, kvh_count)
         return remote(
-            gq_v.at[pl.ds(pl.multiple_of(peer * part, part), part), pl.ds(c * cols, cols)],
+            gq_v.at[pl.ds(pl.multiple_of(peer * part, part), part), pl.ds(pl.multiple_of(c * cols, cols), cols)],
             gq_out.at[:, pl.ds(pl.multiple_of(head * width + c * cols, cols), cols)],
             gq_send.at[c, r - 1],
             gq_recv.at[c, r - 1],
@@ -163,8 +163,9 @@
         copy.wait()
 
     def transpose(rows, columns):
-        for h in range(GROUP):
-            at = slice(h * HD, (h + 1) * HD)
+        @pl.loop(0, GROUP)
+        def _(h):
+            at = pl.ds(pl.multiple_of(h * HD, HD), HD)
             columns[:, at] = rows[:, at].astype(f32).T.astype(bf16)
 
     def send_rows(make, own_rows, out, first):
@@ -209,6 +210,12 @@
             def _(j=j, d=d):
                 term_copy(i, j, d).start()
 
+    def chunk(c):
+        return pl.ds(pl.multiple_of(c * lanes, lanes), lanes)
+
+    def one_head(c, i):
+        return pl.ds(pl.multiple_of((c * PAIR + i) * HD, HD), HD)
+
     def by_rows(ref):
         return jnp.concatenate([ref[:, h * HD : (h + 1) * HD] for h in range(GROUP)], axis=0)
 
@@ -217,8 +224,10 @@
     query_at = lax.rem(lax.broadcasted_iota(jnp.int32, (KBLK, lanes), 1), QBLK)
     causal = key_at <= query_at
     hidden = [jnp.full((KBLK, lanes), count <= j) for j in range(1, slots)]
-    for c in range(chunks):
-        at = slice(c * lanes, (c + 1) * lanes)
+
+    @pl.loop(0, chunks)
+    def _(c):
+        at = chunk(c)
         s = dot(k_all, q_t[:, at], NN)
         s = jnp.concatenate(
             [jnp.where(causal, s[0:KBLK], -1e30)]
@@ -233,35 +242,39 @@
         p = e * (1.0 / jnp.sum(e, axis=0, keepdims=True))
         prob[:, at] = p
         prob_half[:, at] = p.astype(bf16)
+
     send_terms(1, dot(prob_half[...], by_rows(u_v), NN))
 
     v_all = receive(v_copy, v_own, v_in, vals)
-    for c in range(chunks):
-        at = slice(c * lanes, (c + 1) * lanes)
+
+    @pl.loop(0, chunks)
+    def _(c):
+        at = chunk(c)
         dp = dot(v_all, u_t[:, at], NN)
         p = prob[:, at]
         row_term = jnp.sum(p * dp, axis=0, keepdims=True)
         ds = (p * (dp - row_term)).astype(bf16)
         grad_scores[:, at] = ds
+
     send_terms(0, dot(grad_scores[...], by_rows(q_v), NN) * score_scale)
 
     k_t = k_all.astype(f32).T.astype(bf16)
-    for c in range(chunks):
-        at = slice(c * lanes, (c + 1) * lanes)
-        gq_c = dot(k_t, grad_scores[:, at], NN) * score_scale
+
+    @pl.loop(0, chunks)
+    def _(c):
+        gq_c = dot(k_t, grad_scores[:, chunk(c)], NN) * score_scale
         for i in range(PAIR):
-            h = c * PAIR + i
-            gq_v[:, h * HD : (h + 1) * HD] = gq_c[:, i * QBLK : (i + 1) * QBLK].T.astype(bf16)
+            gq_v[:, one_head(c, i)] = gq_c[:, i * QBLK : (i + 1) * QBLK].T.astype(bf16)
         for r in range(1, kvh_count):
             gq_copy(c, r).start()
 
     v_t = v_all.astype(f32).T.astype(bf16)
-    for c in range(chunks):
-        at = slice(c * lanes, (c + 1) * lanes)
-        att_c = dot(v_t, prob_half[:, at], NN)
+
+    @pl.loop(0, chunks)
+    def _(c):
+        att_c = dot(v_t, prob_half[:, chunk(c)], NN)
         for i in range(PAIR):
-            h = c * PAIR + i
-            att_v[:, h * HD : (h + 1) * HD] = att_c[:, i * QBLK : (i + 1) * QBLK].T.astype(bf16)
+            att_v[:, one_head(c, i)] = att_c[:, i * QBLK : (i + 1) * QBLK].T.astype(bf16)
 
     stores = [
         pltpu.make_async_copy(

time: 18.6 us -> 19.8 us (1.065)
  Pallas kernels: 17.2 us -> 18.4 us
    pallas_call x1, Pallas kernels: 16.3 us -> 17.5 us  [on_device(): pl.pallas_call(functools.partial(kernel, ctx_count, kvh_count, distances)...]
where the time goes in v5:
time: 19.8 us; the launch traced here: 19.6 us
  Pallas kernels  18.4 us (93%)
  between operations  1.29 us (7%)
    pallas_call x1, Pallas kernels, on_device(): pl.pallas_call(functools.partial(kernel, ctx_count, kvh_count, distances)...  17.5 us
    pallas_call x1, Pallas kernels, on_device(): pl.pallas_call(functools.partial(finish, ctx_count, distances), out_shape...  0.86 us

profile of v5, /device:TPU:0, one launch (start us, length us, event | category | flops | bytes accessed | tf_op | source)
XLA Modules:
  0.0 19.6 jit_solution(6995392691162138987)
XLA Ops:
  1.3 17.5 %shard_map.93 = (bf16[128,1024]{1,0:T(8,128)(2,1)S(1)}, bf16[32,4096]{1,0:T(8,128)(2,1)S(1)}, f32[2,64,128]{2,1,0:T(8,128)S(1)}, bf16[2,3,64,128]{3,2,1,0:T(8,128)(2,1)S(1)}, s32[3,8,128]{2,1,0:T(8,128)S(1)}) custom-call(s32[1]{0:T(128)S(6)} %copy.10.cnt_ref, s32[1,8]{1,0:T(1,128)} %sel_hbm.1, bf16[128,1024]{1,0:T(8,128)(2,1)} %q_hbm.1, ...), custom_call_target="tpu_custom_call" | custom-call | tf_op jit(solution)/shard_map/pallas_call | solution.py:366
  18.8 0.9 %shard_map.94 = (bf16[128,1024]{1,0:T(8,128)(2,1)}, bf16[32,4096]{1,0:T(8,128)(2,1)}, f32[128,128]{1,0:T(8,128)}, f32[128,128]{1,0:T(8,128)}) custom-call(bf16[128,1024]{1,0:T(8,128)(2,1)S(1)} %get-tuple-element.9.att, bf16[32,4096]{1,0:T(8,128)(2,1)S(1)} %get-tuple-element.10.gq, f32[2,64,128]{2,1,0:T(8,128)S(1)} %get-tuple-element.11.own, ...), custom_call_target="tpu_custom_call" | custom-call | tf_op jit(solution)/shard_map/pallas_call | solution.py:420

commit v6 on v4

--- a/solution.py
+++ b/solution.py
@@ -18,6 +18,7 @@
 MESH = pl.DeviceIdType.MESH
 LOG2E = math.log2(math.e)
 NN = (((1,), (0,)), ((), ()))
+NT = (((1,), (1,)), ((), ()))
 
 
 def dot(a, b, dims):
@@ -39,18 +40,14 @@
     own_out,
     terms_in,
     sel_store,
-    sel_ref,
     q_v,
     u_v,
-    q_t,
-    u_t,
     k_own,
     v_own,
     k_out,
     v_out,
     k_in,
     v_in,
-    sel_out,
     sel_in,
     keys,
     vals,
@@ -86,7 +83,6 @@
         pltpu.make_async_copy(src, dst, load_sem.at[i])
         for i, (src, dst) in enumerate(
             [
-                (sel_hbm, sel_ref),
                 (k_hbm, k_own),
                 (v_hbm, v_own),
                 (q_hbm, q_v),
@@ -111,11 +107,6 @@
         def _():
             pl.semaphore_signal(barrier, inc=1, device_id={"ctx": me - d}, device_id_type=MESH)
 
-    for copy in loads[:3]:
-        copy.wait()
-    for j, d in enumerate(distances):
-        sel_out[j] = jnp.full((8, HD), sel_ref[0, j + 1] - 2 * (me - d), jnp.int32)
-
     partners = kvh_count - 1
     for d in distances:
         partners += 1 - (me + d) // ctx_count + (me - d + ctx_count) // ctx_count
@@ -134,7 +125,7 @@
         return remote(v_out.at[j], v_in.at[j], kv_send.at[1, j], kv_recv.at[1, j], ctx=me + d)
 
     def sel_copy(j, d):
-        return remote(sel_out.at[j], sel_in.at[j], sel_send.at[j], sel_recv.at[j], ctx=me - d)
+        return remote(sel_hbm, sel_in.at[j], sel_send.at[j], sel_recv.at[j], ctx=me - d)
 
     def term_copy(i, j, d):
         return remote(
@@ -159,13 +150,8 @@
         def _(j=j, d=d):
             sel_copy(j, d).start()
 
-    for copy in loads[3:]:
+    for copy in loads:
         copy.wait()
-
-    def transpose(rows, columns):
-        for h in range(GROUP):
-            at = slice(h * HD, (h + 1) * HD)
-            columns[:, at] = rows[:, at].astype(f32).T.astype(bf16)
 
     def send_rows(make, own_rows, out, first):
         for j, d in enumerate(distances):
@@ -174,16 +160,14 @@
             def _(j=j, d=d):
                 if first:
                     sel_copy(j, d).wait_recv()
-                upper = jnp.broadcast_to(sel_in[j, 0:1], (KBLK, HD)) > 0
+                upper = jnp.broadcast_to(sel_in[j, :, j + 1 : j + 2], (KBLK, HD)) > 2 * me
                 lo = own_rows[0:KBLK].astype(f32)
                 hi = own_rows[KBLK : 2 * KBLK].astype(f32)
                 out[j] = jnp.where(upper, hi, lo).astype(bf16)
                 make(j, d).start()
 
-    transpose(q_v, q_t)
     send_rows(k_copy, k_own, k_out, True)
     send_rows(v_copy, v_own, v_out, False)
-    transpose(u_v, u_t)
 
     count = cnt_ref[0]
 
@@ -211,6 +195,9 @@
 
     def by_rows(ref):
         return jnp.concatenate([ref[:, h * HD : (h + 1) * HD] for h in range(GROUP)], axis=0)
+
+    q_rows = by_rows(q_v)
+    u_rows = by_rows(u_v)
 
     k_all = receive(k_copy, k_own, k_in, keys)
     key_at = lax.broadcasted_iota(jnp.int32, (KBLK, lanes), 0)
@@ -219,7 +206,7 @@
     hidden = [jnp.full((KBLK, lanes), count <= j) for j in range(1, slots)]
     for c in range(chunks):
         at = slice(c * lanes, (c + 1) * lanes)
-        s = dot(k_all, q_t[:, at], NN)
+        s = dot(k_all, q_rows[at], NT)
         s = jnp.concatenate(
             [jnp.where(causal, s[0:KBLK], -1e30)]
             + [
@@ -233,17 +220,17 @@
         p = e * (1.0 / jnp.sum(e, axis=0, keepdims=True))
         prob[:, at] = p
         prob_half[:, at] = p.astype(bf16)
-    send_terms(1, dot(prob_half[...], by_rows(u_v), NN))
+    send_terms(1, dot(prob_half[...], u_rows, NN))
 
     v_all = receive(v_copy, v_own, v_in, vals)
     for c in range(chunks):
         at = slice(c * lanes, (c + 1) * lanes)
-        dp = dot(v_all, u_t[:, at], NN)
+        dp = dot(v_all, u_rows[at], NT)
         p = prob[:, at]
         row_term = jnp.sum(p * dp, axis=0, keepdims=True)
         ds = (p * (dp - row_term)).astype(bf16)
         grad_scores[:, at] = ds
-    send_terms(0, dot(grad_scores[...], by_rows(q_v), NN) * score_scale)
+    send_terms(0, dot(grad_scores[...], q_rows, NN) * score_scale)
 
     k_t = k_all.astype(f32).T.astype(bf16)
     for c in range(chunks):
@@ -315,7 +302,7 @@
 
         @pl.when(me + d < ctx_count)
         def _(j=j, d=d):
-            where = jnp.broadcast_to(sel[j, 0:1], (KBLK, HD))
+            where = jnp.broadcast_to(sel[j, :, j + 1 : j + 2], (KBLK, HD)) - 2 * me
             for i in range(2):
                 term = terms[i, j].astype(jnp.float32)
                 total[i, 0:KBLK] += jnp.where(where == 0, term, 0.0)
@@ -356,24 +343,20 @@
             + [
                 jax.ShapeDtypeStruct((2, KBLK, HD), f32),
                 jax.ShapeDtypeStruct((2, far, KBLK, HD), bf16),
-                jax.ShapeDtypeStruct((far, 8, HD), jnp.int32),
+                jax.ShapeDtypeStruct((far, 1, SLOTS), jnp.int32),
             ],
             in_specs=[smem] + [hbm] * 5,
             out_specs=[anywhere] * 5,
             scratch_shapes=[
-                pltpu.SMEM((1, SLOTS), jnp.int32),
                 pltpu.VMEM((tokens, width), bf16),
                 pltpu.VMEM((tokens, width), bf16),
-                pltpu.VMEM((HD, GROUP * tokens), bf16),
-                pltpu.VMEM((HD, GROUP * tokens), bf16),
                 pltpu.VMEM((key_rows, HD), bf16),
                 pltpu.VMEM((key_rows, HD), bf16),
                 pltpu.VMEM((far, KBLK, HD), bf16),
                 pltpu.VMEM((far, KBLK, HD), bf16),
                 pltpu.VMEM((far, KBLK, HD), bf16),
                 pltpu.VMEM((far, KBLK, HD), bf16),
-                pltpu.VMEM((far, 8, HD), jnp.int32),
-                pltpu.VMEM((far, 8, HD), jnp.int32),
+                pltpu.VMEM((far, 1, SLOTS), jnp.int32),
                 pltpu.VMEM((slots * KBLK, HD), bf16),
                 pltpu.VMEM((slots * KBLK, HD), bf16),
                 pltpu.VMEM((slots * KBLK, GROUP * tokens), f32),
@@ -383,7 +366,7 @@
                 pltpu.VMEM((tokens, width), bf16),
                 pltpu.VMEM((2, KBLK, HD), f32),
                 pltpu.VMEM((2, far, KBLK, HD), bf16),
-                dma((5,)),
+                dma((4,)),
                 dma((4,)),
                 dma((2, far)),
                 dma((2, far)),

time: 18.6 us -> 18.8 us (1.011)
  Pallas kernels: 17.2 us -> 17.4 us
where the time goes in v6:
time: 18.8 us; the launch traced here: 18.7 us
  Pallas kernels  17.4 us (93%)
  between operations  1.29 us (7%)
    pallas_call x1, Pallas kernels, on_device(): pl.pallas_call(functools.partial(kernel, ctx_count, kvh_count, distances)...  16.5 us
    pallas_call x1, Pallas kernels, on_device(): pl.pallas_call(functools.partial(finish, ctx_count, distances), out_shape...  0.94 us

profile of v6, /device:TPU:0, one launch (start us, length us, event | category | flops | bytes accessed | tf_op | source)
XLA Modules:
  0.0 18.7 jit_solution(12108575589390407908)
XLA Ops:
  1.3 16.5 %shard_map.93 = (bf16[128,1024]{1,0:T(8,128)(2,1)S(1)}, bf16[32,4096]{1,0:T(8,128)(2,1)S(1)}, f32[2,64,128]{2,1,0:T(8,128)S(1)}, bf16[2,3,64,128]{3,2,1,0:T(8,128)(2,1)S(1)}, s32[3,1,8]{2,1,0:T(1,128)S(1)}) custom-call(s32[1]{0:T(128)S(6)} %copy.10.cnt_ref, s32[1,8]{1,0:T(1,128)} %sel_hbm.1, bf16[128,1024]{1,0:T(8,128)(2,1)} %q_hbm.1, ...), custom_call_target="tpu_custom_call" | custom-call | tf_op jit(solution)/shard_map/pallas_call | solution.py:340
  17.7 0.9 %shard_map.94 = (bf16[128,1024]{1,0:T(8,128)(2,1)}, bf16[32,4096]{1,0:T(8,128)(2,1)}, f32[128,128]{1,0:T(8,128)}, f32[128,128]{1,0:T(8,128)}) custom-call(bf16[128,1024]{1,0:T(8,128)(2,1)S(1)} %get-tuple-element.9.att, bf16[32,4096]{1,0:T(8,128)(2,1)S(1)} %get-tuple-element.10.gq, f32[2,64,128]{2,1,0:T(8,128)S(1)} %get-tuple-element.11.own, ...), custom_call_target="tpu_custom_call" | custom-call | tf_op jit(solution)/shard_map/pallas_call | solution.py:390

commit v7 on v6

--- a/solution.py
+++ b/solution.py
@@ -51,7 +51,8 @@
     sel_in,
     keys,
     vals,
-    prob,
+    expon,
+    grad_probs,
     prob_half,
     grad_scores,
     att_v,
@@ -166,23 +167,59 @@
                 out[j] = jnp.where(upper, hi, lo).astype(bf16)
                 make(j, d).start()
 
+    count = cnt_ref[0]
+    key_at = lax.broadcasted_iota(jnp.int32, (KBLK, lanes), 0)
+    query_at = lax.rem(lax.broadcasted_iota(jnp.int32, (KBLK, lanes), 1), QBLK)
+    causal = key_at <= query_at
+    every = [(c, slice(c * lanes, (c + 1) * lanes)) for c in range(chunks)]
+
+    def slot_rows(j):
+        return slice(j * KBLK, (j + 1) * KBLK)
+
+    def heads_of(ref, c):
+        return jnp.concatenate(
+            [ref[:, h * HD : (h + 1) * HD] for h in range(c * PAIR, (c + 1) * PAIR)], axis=0
+        )
+
+    def receive(j, make, arrived, chosen):
+        d = distances[j - 1]
+
+        @pl.when(me - d >= 0)
+        def _():
+            make(j - 1, d).wait_recv()
+
+        live = jnp.full((KBLK, HD), count > j)
+        rows = jnp.where(live, arrived[j - 1].astype(f32), 0.0)
+        chosen[slot_rows(j)] = rows.astype(bf16)
+
+    peaks, sums, dots = {}, {}, {}
+
+    def slot_scores(j):
+        rows = keys[slot_rows(j)]
+        for c, at in every:
+            s = dot(rows, heads_of(q_v, c), NT)
+            if j == 0:
+                s = jnp.where(causal, s, -1e30)
+            peak = jnp.max(s, axis=0, keepdims=True)
+            e = jnp.exp2((s - peak) * (score_scale * LOG2E))
+            expon[slot_rows(j), at] = e
+            sums[j, c] = jnp.sum(e, axis=0, keepdims=True)
+            peaks[j, c] = peak
+            if j > 0:
+                peaks[j, c] = jnp.where(jnp.full((1, lanes), count > j), peak, -1e30)
+
+    def slot_grads(j):
+        rows = vals[slot_rows(j)]
+        for c, at in every:
+            dp = dot(rows, heads_of(u_v, c), NT)
+            grad_probs[slot_rows(j), at] = dp
+            dots[j, c] = jnp.sum(expon[slot_rows(j), at] * dp, axis=0, keepdims=True)
+
+    keys[slot_rows(0)] = k_own[0:KBLK]
+    vals[slot_rows(0)] = v_own[0:KBLK]
+    slot_scores(0)
     send_rows(k_copy, k_own, k_out, True)
     send_rows(v_copy, v_own, v_out, False)
-
-    count = cnt_ref[0]
-
-    def receive(make, own_rows, arrived, chosen):
-        chosen[0:KBLK] = own_rows[0:KBLK]
-        for j, d in enumerate(distances):
-
-            @pl.when(me - d >= 0)
-            def _(j=j, d=d):
-                make(j, d).wait_recv()
-
-            live = jnp.full((KBLK, HD), count > j + 1)
-            rows = jnp.where(live, arrived[j].astype(f32), 0.0)
-            chosen[(j + 1) * KBLK : (j + 2) * KBLK] = rows.astype(bf16)
-        return chosen[...]
 
     def send_terms(i, term):
         own[i] = term[0:KBLK]
@@ -196,43 +233,37 @@
     def by_rows(ref):
         return jnp.concatenate([ref[:, h * HD : (h + 1) * HD] for h in range(GROUP)], axis=0)
 
-    q_rows = by_rows(q_v)
-    u_rows = by_rows(u_v)
-
-    k_all = receive(k_copy, k_own, k_in, keys)
-    key_at = lax.broadcasted_iota(jnp.int32, (KBLK, lanes), 0)
-    query_at = lax.rem(lax.broadcasted_iota(jnp.int32, (KBLK, lanes), 1), QBLK)
-    causal = key_at <= query_at
-    hidden = [jnp.full((KBLK, lanes), count <= j) for j in range(1, slots)]
-    for c in range(chunks):
-        at = slice(c * lanes, (c + 1) * lanes)
-        s = dot(k_all, q_rows[at], NT)
-        s = jnp.concatenate(
-            [jnp.where(causal, s[0:KBLK], -1e30)]
-            + [
-                jnp.where(hidden[j - 1], -1e30, s[j * KBLK : (j + 1) * KBLK])
-                for j in range(1, slots)
-            ],
-            axis=0,
-        )
-        peak = jnp.max(s, axis=0, keepdims=True)
-        e = jnp.exp2((s - peak) * (score_scale * LOG2E))
-        p = e * (1.0 / jnp.sum(e, axis=0, keepdims=True))
-        prob[:, at] = p
-        prob_half[:, at] = p.astype(bf16)
-    send_terms(1, dot(prob_half[...], u_rows, NN))
-
-    v_all = receive(v_copy, v_own, v_in, vals)
-    for c in range(chunks):
-        at = slice(c * lanes, (c + 1) * lanes)
-        dp = dot(v_all, u_rows[at], NT)
-        p = prob[:, at]
-        row_term = jnp.sum(p * dp, axis=0, keepdims=True)
-        ds = (p * (dp - row_term)).astype(bf16)
-        grad_scores[:, at] = ds
-    send_terms(0, dot(grad_scores[...], q_rows, NN) * score_scale)
-
-    k_t = k_all.astype(f32).T.astype(bf16)
+    slot_grads(0)
+    for j in range(1, slots):
+        receive(j, k_copy, k_in, keys)
+        slot_scores(j)
+
+    shares = {}
+    for c, at in every:
+        peak = functools.reduce(jnp.maximum, [peaks[j, c] for j in range(slots)])
+        scale = [
+            jnp.exp2((peaks[j, c] - peak) * (score_scale * LOG2E)) for j in range(slots)
+        ]
+        inverse = 1.0 / sum(scale[j] * sums[j, c] for j in range(slots))
+        for j in range(slots):
+            shares[j, c] = scale[j] * inverse
+            p = expon[slot_rows(j), at] * shares[j, c]
+            prob_half[slot_rows(j), at] = p.astype(bf16)
+    send_terms(1, dot(prob_half[...], by_rows(u_v), NN))
+
+    for j in range(1, slots):
+        receive(j, v_copy, v_in, vals)
+        slot_grads(j)
+
+    for c, at in every:
+        row_term = sum(shares[j, c] * dots[j, c] for j in range(slots))
+        for j in range(slots):
+            p = expon[slot_rows(j), at] * shares[j, c]
+            ds = p * (grad_probs[slot_rows(j), at] - row_term)
+            grad_scores[slot_rows(j), at] = ds.astype(bf16)
+    send_terms(0, dot(grad_scores[...], by_rows(q_v), NN) * score_scale)
+
+    k_t = keys[...].astype(f32).T.astype(bf16)
     for c in range(chunks):
         at = slice(c * lanes, (c + 1) * lanes)
         gq_c = dot(k_t, grad_scores[:, at], NN) * score_scale
@@ -242,7 +273,7 @@
         for r in range(1, kvh_count):
             gq_copy(c, r).start()
 
-    v_t = v_all.astype(f32).T.astype(bf16)
+    v_t = vals[...].astype(f32).T.astype(bf16)
     for c in range(chunks):
         at = slice(c * lanes, (c + 1) * lanes)
         att_c = dot(v_t, prob_half[:, at], NN)
@@ -360,6 +391,7 @@
                 pltpu.VMEM((slots * KBLK, HD), bf16),
                 pltpu.VMEM((slots * KBLK, HD), bf16),
                 pltpu.VMEM((slots * KBLK, GROUP * tokens), f32),
+                pltpu.VMEM((slots * KBLK, GROUP * tokens), f32),
                 pltpu.VMEM((slots * KBLK, GROUP * tokens), bf16),
                 pltpu.VMEM((slots * KBLK, GROUP * tokens), bf16),
                 pltpu.VMEM((tokens, width), bf16),

time: 18.8 us -> 19.1 us (1.016)
  Pallas kernels: 17.4 us -> 17.7 us
    pallas_call x1, Pallas kernels: 16.5 us -> 16.8 us  [on_device(): pl.pallas_call(functools.partial(kernel, ctx_count, kvh_count, distances)...]
where the time goes in v7:
time: 19.1 us; the launch traced here: 19 us
  Pallas kernels  17.7 us (93%)
  between operations  1.29 us (7%)
    pallas_call x1, Pallas kernels, on_device(): pl.pallas_call(functools.partial(kernel, ctx_count, kvh_count, distances)...  16.8 us
    pallas_call x1, Pallas kernels, on_device(): pl.pallas_call(functools.partial(finish, ctx_count, distances), out_shape...  0.94 us

profile of v7, /device:TPU:0, one launch (start us, length us, event | category | flops | bytes accessed | tf_op | source)
XLA Modules:
  0.0 19.0 jit_solution(1658931163214862171)
XLA Ops:
  1.3 16.8 %shard_map.93 = (bf16[128,1024]{1,0:T(8,128)(2,1)S(1)}, bf16[32,4096]{1,0:T(8,128)(2,1)S(1)}, f32[2,64,128]{2,1,0:T(8,128)S(1)}, bf16[2,3,64,128]{3,2,1,0:T(8,128)(2,1)S(1)}, s32[3,1,8]{2,1,0:T(1,128)S(1)}) custom-call(s32[1]{0:T(128)S(6)} %copy.10.cnt_ref, s32[1,8]{1,0:T(1,128)} %sel_hbm.1, bf16[128,1024]{1,0:T(8,128)(2,1)} %q_hbm.1, ...), custom_call_target="tpu_custom_call" | custom-call | tf_op jit(solution)/shard_map/pallas_call | solution.py:371
  18.0 0.9 %shard_map.94 = (bf16[128,1024]{1,0:T(8,128)(2,1)}, bf16[32,4096]{1,0:T(8,128)(2,1)}, f32[128,128]{1,0:T(8,128)}, f32[128,128]{1,0:T(8,128)}) custom-call(bf16[128,1024]{1,0:T(8,128)(2,1)S(1)} %get-tuple-element.9.att, bf16[32,4096]{1,0:T(8,128)(2,1)S(1)} %get-tuple-element.10.gq, f32[2,64,128]{2,1,0:T(8,128)S(1)} %get-tuple-element.11.own, ...), custom_call_target="tpu_custom_call" | custom-call | tf_op jit(solution)/shard_map/pallas_call | solution.py:422

commit v8 on v7

--- a/solution.py
+++ b/solution.py
@@ -217,7 +217,6 @@
 
     keys[slot_rows(0)] = k_own[0:KBLK]
     vals[slot_rows(0)] = v_own[0:KBLK]
-    slot_scores(0)
     send_rows(k_copy, k_own, k_out, True)
     send_rows(v_copy, v_own, v_out, False)
 
@@ -233,6 +232,7 @@
     def by_rows(ref):
         return jnp.concatenate([ref[:, h * HD : (h + 1) * HD] for h in range(GROUP)], axis=0)
 
+    slot_scores(0)
     slot_grads(0)
     for j in range(1, slots):
         receive(j, k_copy, k_in, keys)
@@ -255,23 +255,30 @@
         receive(j, v_copy, v_in, vals)
         slot_grads(j)
 
-    for c, at in every:
+    k_t = keys[...].astype(f32).T.astype(bf16)
+
+    def score_gradients(c, at):
         row_term = sum(shares[j, c] * dots[j, c] for j in range(slots))
         for j in range(slots):
             p = expon[slot_rows(j), at] * shares[j, c]
             ds = p * (grad_probs[slot_rows(j), at] - row_term)
             grad_scores[slot_rows(j), at] = ds.astype(bf16)
-    send_terms(0, dot(grad_scores[...], by_rows(q_v), NN) * score_scale)
-
-    k_t = keys[...].astype(f32).T.astype(bf16)
-    for c in range(chunks):
-        at = slice(c * lanes, (c + 1) * lanes)
+
+    def query_gradients(c, at):
         gq_c = dot(k_t, grad_scores[:, at], NN) * score_scale
         for i in range(PAIR):
             h = c * PAIR + i
             gq_v[:, h * HD : (h + 1) * HD] = gq_c[:, i * QBLK : (i + 1) * QBLK].T.astype(bf16)
         for r in range(1, kvh_count):
             gq_copy(c, r).start()
+
+    score_gradients(*every[0])
+    query_gradients(*every[0])
+    for c, at in every[1:]:
+        score_gradients(c, at)
+    send_terms(0, dot(grad_scores[...], by_rows(q_v), NN) * score_scale)
+    for c, at in every[1:]:
+        query_gradients(c, at)
 
     v_t = vals[...].astype(f32).T.astype(bf16)
     for c in range(chunks):

time: 19.1 us -> 19.4 us (1.016)
  Pallas kernels: 17.7 us -> 17.9 us
    pallas_call x1, Pallas kernels: 16.8 us -> 17 us  [on_device(): pl.pallas_call(functools.partial(kernel, ctx_count, kvh_count, distances)...]
where the time goes in v8:
time: 19.4 us; the launch traced here: 19.2 us
  Pallas kernels  17.9 us (92%)
  between operations  1.29 us (7%)
    pallas_call x1, Pallas kernels, on_device(): pl.pallas_call(functools.partial(kernel, ctx_count, kvh_count, distances)...  17 us
    pallas_call x1, Pallas kernels, on_device(): pl.pallas_call(functools.partial(finish, ctx_count, distances), out_shape...  0.94 us

profile of v8, /device:TPU:0, one launch (start us, length us, event | category | flops | bytes accessed | tf_op | source)
XLA Modules:
  0.0 19.2 jit_solution(4446094784175662137)
XLA Ops:
  1.3 17.0 %shard_map.93 = (bf16[128,1024]{1,0:T(8,128)(2,1)S(1)}, bf16[32,4096]{1,0:T(8,128)(2,1)S(1)}, f32[2,64,128]{2,1,0:T(8,128)S(1)}, bf16[2,3,64,128]{3,2,1,0:T(8,128)(2,1)S(1)}, s32[3,1,8]{2,1,0:T(1,128)S(1)}) custom-call(s32[1]{0:T(128)S(6)} %copy.10.cnt_ref, s32[1,8]{1,0:T(1,128)} %sel_hbm.1, bf16[128,1024]{1,0:T(8,128)(2,1)} %q_hbm.1, ...), custom_call_target="tpu_custom_call" | custom-call | tf_op jit(solution)/shard_map/pallas_call | solution.py:378
  18.3 0.9 %shard_map.94 = (bf16[128,1024]{1,0:T(8,128)(2,1)}, bf16[32,4096]{1,0:T(8,128)(2,1)}, f32[128,128]{1,0:T(8,128)}, f32[128,128]{1,0:T(8,128)}) custom-call(bf16[128,1024]{1,0:T(8,128)(2,1)S(1)} %get-tuple-element.9.att, bf16[32,4096]{1,0:T(8,128)(2,1)S(1)} %get-tuple-element.10.gq, f32[2,64,128]{2,1,0:T(8,128)S(1)} %get-tuple-element.11.own, ...), custom_call_target="tpu_custom_call" | custom-call | tf_op jit(solution)/shard_map/pallas_call | solution.py:429

commit v9 on v6

--- a/solution.py
+++ b/solution.py
@@ -14,6 +14,7 @@
 QBLK = 128
 SLOTS = 8
 PAIR = 2
+SENDS = 2
 
 MESH = pl.DeviceIdType.MESH
 LOG2E = math.log2(math.e)
@@ -44,10 +45,8 @@
     u_v,
     k_own,
     v_own,
-    k_out,
-    v_out,
-    k_in,
-    v_in,
+    kv_out,
+    kv_in,
     sel_in,
     keys,
     vals,
@@ -118,11 +117,8 @@
             device_id=where, device_id_type=MESH,
         )
 
-    def k_copy(j, d):
-        return remote(k_out.at[j], k_in.at[j], kv_send.at[0, j], kv_recv.at[0, j], ctx=me + d)
-
-    def v_copy(j, d):
-        return remote(v_out.at[j], v_in.at[j], kv_send.at[1, j], kv_recv.at[1, j], ctx=me + d)
+    def kv_copy(j, d):
+        return remote(kv_out.at[j], kv_in.at[j], kv_send.at[j], kv_recv.at[j], ctx=me + d)
 
     def sel_copy(j, d):
         return remote(sel_hbm, sel_in.at[j], sel_send.at[j], sel_recv.at[j], ctx=me - d)
@@ -133,7 +129,7 @@
         )
 
     def gq_copy(c, r):
-        cols = PAIR * HD
+        cols = width // SENDS
         peer = lax.rem(head + r, kvh_count)
         return remote(
             gq_v.at[pl.ds(pl.multiple_of(peer * part, part), part), pl.ds(c * cols, cols)],
@@ -153,36 +149,19 @@
     for copy in loads:
         copy.wait()
 
-    def send_rows(make, own_rows, out, first):
-        for j, d in enumerate(distances):
-
-            @pl.when(me + d < ctx_count)
-            def _(j=j, d=d):
-                if first:
-                    sel_copy(j, d).wait_recv()
-                upper = jnp.broadcast_to(sel_in[j, :, j + 1 : j + 2], (KBLK, HD)) > 2 * me
+    for j, d in enumerate(distances):
+
+        @pl.when(me + d < ctx_count)
+        def _(j=j, d=d):
+            sel_copy(j, d).wait_recv()
+            upper = jnp.broadcast_to(sel_in[j, :, j + 1 : j + 2], (KBLK, HD)) > 2 * me
+            for i, own_rows in enumerate((k_own, v_own)):
                 lo = own_rows[0:KBLK].astype(f32)
                 hi = own_rows[KBLK : 2 * KBLK].astype(f32)
-                out[j] = jnp.where(upper, hi, lo).astype(bf16)
-                make(j, d).start()
-
-    send_rows(k_copy, k_own, k_out, True)
-    send_rows(v_copy, v_own, v_out, False)
+                kv_out[j, i * KBLK : (i + 1) * KBLK] = jnp.where(upper, hi, lo).astype(bf16)
+            kv_copy(j, d).start()
 
     count = cnt_ref[0]
-
-    def receive(make, own_rows, arrived, chosen):
-        chosen[0:KBLK] = own_rows[0:KBLK]
-        for j, d in enumerate(distances):
-
-            @pl.when(me - d >= 0)
-            def _(j=j, d=d):
-                make(j, d).wait_recv()
-
-            live = jnp.full((KBLK, HD), count > j + 1)
-            rows = jnp.where(live, arrived[j].astype(f32), 0.0)
-            chosen[(j + 1) * KBLK : (j + 2) * KBLK] = rows.astype(bf16)
-        return chosen[...]
 
     def send_terms(i, term):
         own[i] = term[0:KBLK]
@@ -199,7 +178,20 @@
     q_rows = by_rows(q_v)
     u_rows = by_rows(u_v)
 
-    k_all = receive(k_copy, k_own, k_in, keys)
+    keys[0:KBLK] = k_own[0:KBLK]
+    vals[0:KBLK] = v_own[0:KBLK]
+    for j, d in enumerate(distances):
+
+        @pl.when(me - d >= 0)
+        def _(j=j, d=d):
+            kv_copy(j, d).wait_recv()
+
+        live = jnp.full((KBLK, HD), count > j + 1)
+        for i, chosen in enumerate((keys, vals)):
+            rows = kv_in[j, i * KBLK : (i + 1) * KBLK].astype(f32)
+            chosen[(j + 1) * KBLK : (j + 2) * KBLK] = jnp.where(live, rows, 0.0).astype(bf16)
+    k_all = keys[...]
+    v_all = vals[...]
     key_at = lax.broadcasted_iota(jnp.int32, (KBLK, lanes), 0)
     query_at = lax.rem(lax.broadcasted_iota(jnp.int32, (KBLK, lanes), 1), QBLK)
     causal = key_at <= query_at
@@ -222,7 +214,6 @@
         prob_half[:, at] = p.astype(bf16)
     send_terms(1, dot(prob_half[...], u_rows, NN))
 
-    v_all = receive(v_copy, v_own, v_in, vals)
     for c in range(chunks):
         at = slice(c * lanes, (c + 1) * lanes)
         dp = dot(v_all, u_rows[at], NT)
@@ -239,8 +230,9 @@
         for i in range(PAIR):
             h = c * PAIR + i
             gq_v[:, h * HD : (h + 1) * HD] = gq_c[:, i * QBLK : (i + 1) * QBLK].T.astype(bf16)
-        for r in range(1, kvh_count):
-            gq_copy(c, r).start()
+        if (c + 1) * SENDS % chunks == 0:
+            for r in range(1, kvh_count):
+                gq_copy((c + 1) * SENDS // chunks - 1, r).start()
 
     v_t = v_all.astype(f32).T.astype(bf16)
     for c in range(chunks):
@@ -267,8 +259,7 @@
 
         @pl.when(me + d < ctx_count)
         def _(j=j, d=d):
-            k_copy(j, d).wait_send()
-            v_copy(j, d).wait_send()
+            kv_copy(j, d).wait_send()
             term_copy(1, j, d).wait_recv()
             term_copy(0, j, d).wait_recv()
 
@@ -278,7 +269,7 @@
             term_copy(1, j, d).wait_send()
             term_copy(0, j, d).wait_send()
 
-    for c in range(chunks):
+    for c in range(SENDS):
         for r in range(1, kvh_count):
             gq_copy(c, r).wait()
     for copy in stores:
@@ -325,7 +316,6 @@
         tokens, width = queries.shape
         key_rows = keys.shape[0]
         assert tokens == QBLK and key_rows == 2 * KBLK and selected.shape[0] == 1
-        chunks = GROUP // PAIR
         bf16, f32 = jnp.bfloat16, jnp.float32
         dma = pltpu.SemaphoreType.DMA
         smem = pl.BlockSpec(memory_space=pltpu.SMEM)
@@ -352,10 +342,8 @@
                 pltpu.VMEM((tokens, width), bf16),
                 pltpu.VMEM((key_rows, HD), bf16),
                 pltpu.VMEM((key_rows, HD), bf16),
-                pltpu.VMEM((far, KBLK, HD), bf16),
-                pltpu.VMEM((far, KBLK, HD), bf16),
-                pltpu.VMEM((far, KBLK, HD), bf16),
-                pltpu.VMEM((far, KBLK, HD), bf16),
+                pltpu.VMEM((far, 2 * KBLK, HD), bf16),
+                pltpu.VMEM((far, 2 * KBLK, HD), bf16),
                 pltpu.VMEM((far, 1, SLOTS), jnp.int32),
                 pltpu.VMEM((slots * KBLK, HD), bf16),
                 pltpu.VMEM((slots * KBLK, HD), bf16),
@@ -368,14 +356,14 @@
                 pltpu.VMEM((2, far, KBLK, HD), bf16),
                 dma((4,)),
                 dma((4,)),
-                dma((2, far)),
-                dma((2, far)),
+                dma((far,)),
+                dma((far,)),
                 dma((far,)),
                 dma((far,)),
                 dma((2, far)),
                 dma((2, far)),
-                dma((chunks, kvh_count - 1)),
-                dma((chunks, kvh_count - 1)),
+                dma((SENDS, kvh_count - 1)),
+                dma((SENDS, kvh_count - 1)),
             ],
             compiler_params=pltpu.CompilerParams(
                 collective_id=0, has_side_effects=True, vmem_limit_bytes=32 * 1024 * 1024

time: 18.8 us -> 18.8 us (level)
  no operation moved by 1% of the time
where the time goes in v9:
time: 18.8 us; the launch traced here: 18.6 us
  Pallas kernels  17.3 us (92%)
  between operations  1.29 us (7%)
    pallas_call x1, Pallas kernels, on_device(): pl.pallas_call(functools.partial(kernel, ctx_count, kvh_count, distances)...  16.4 us
    pallas_call x1, Pallas kernels, on_device(): pl.pallas_call(functools.partial(finish, ctx_count, distances), out_shape...  0.94 us

profile of v9, /device:TPU:0, one launch (start us, length us, event | category | flops | bytes accessed | tf_op | source)
XLA Modules:
  0.0 18.6 jit_solution(6977609811737701723)
XLA Ops:
  1.3 16.4 %shard_map.93 = (bf16[128,1024]{1,0:T(8,128)(2,1)S(1)}, bf16[32,4096]{1,0:T(8,128)(2,1)S(1)}, f32[2,64,128]{2,1,0:T(8,128)S(1)}, bf16[2,3,64,128]{3,2,1,0:T(8,128)(2,1)S(1)}, s32[3,1,8]{2,1,0:T(1,128)S(1)}) custom-call(s32[1]{0:T(128)S(6)} %copy.10.cnt_ref, s32[1,8]{1,0:T(1,128)} %sel_hbm.1, bf16[128,1024]{1,0:T(8,128)(2,1)} %q_hbm.1, ...), custom_call_target="tpu_custom_call" | custom-call | tf_op jit(solution)/shard_map/pallas_call | solution.py:330
  17.7 0.9 %shard_map.94 = (bf16[128,1024]{1,0:T(8,128)(2,1)}, bf16[32,4096]{1,0:T(8,128)(2,1)}, f32[128,128]{1,0:T(8,128)}, f32[128,128]{1,0:T(8,128)}) custom-call(bf16[128,1024]{1,0:T(8,128)(2,1)S(1)} %get-tuple-element.9.att, bf16[32,4096]{1,0:T(8,128)(2,1)S(1)} %get-tuple-element.10.gq, f32[2,64,128]{2,1,0:T(8,128)S(1)} %get-tuple-element.11.own, ...), custom_call_target="tpu_custom_call" | custom-call | tf_op jit(solution)/shard_map/pallas_call | solution.py:378

commit v10 on v2

--- a/solution.py
+++ b/solution.py
@@ -224,7 +224,6 @@
     send_terms(1, dot(prob_half[...], by_rows(u_v), NN))
 
     v_all = receive(v_copy, v_own, v_in, vals)
-    k_t = k_all.astype(f32).T.astype(bf16)
     for c in range(chunks):
         at = slice(c * lanes, (c + 1) * lanes)
         dp = dot(v_all, u_t[:, at], NN)
@@ -232,13 +231,17 @@
         row_term = jnp.sum(p * dp, axis=0, keepdims=True)
         ds = (p * (dp - row_term)).astype(bf16)
         grad_scores[:, at] = ds
-        gq_c = dot(k_t, ds, NN) * score_scale
+    send_terms(0, dot(grad_scores[...], by_rows(q_v), NN) * score_scale)
+
+    k_t = k_all.astype(f32).T.astype(bf16)
+    for c in range(chunks):
+        at = slice(c * lanes, (c + 1) * lanes)
+        gq_c = dot(k_t, grad_scores[:, at], NN) * score_scale
         for i in range(PAIR):
             h = c * PAIR + i
             gq_v[:, h * HD : (h + 1) * HD] = gq_c[:, i * QBLK : (i + 1) * QBLK].T.astype(bf16)
         for r in range(1, kvh_count):
             gq_copy(c, r).start()
-    send_terms(0, dot(grad_scores[...], by_rows(q_v), NN) * score_scale)
 
     v_t = v_all.astype(f32).T.astype(bf16)
     for c in range(chunks):
@@ -392,6 +395,7 @@
             in_specs=[anywhere, anywhere, vmem, vmem, vmem],
             out_specs=[hbm] * 4,
             scratch_shapes=[pltpu.VMEM((2, key_rows, HD), f32), dma((4,))],
+            compiler_params=pltpu.CompilerParams(vmem_limit_bytes=4 * 1024 * 1024),
         )(*parts)
 
     placed = (

time: 41.2 us -> 19.4 us (0.47)
  Pallas kernels: 36.5 us -> 17.9 us
  local copies, waits for them, and re-layouts: 3.23 us -> 0 us
    pallas_call x1, Pallas kernels: 17.9 us -> 0.86 us  [on_device(): pl.pallas_call(functools.partial(finish, ctx_count, distances), out_shape...]
    unnamed x10 -> x0, local copies, waits for them, and re-layouts: 3.23 us -> none
    pallas_call x1, Pallas kernels: 18.6 us -> 17.1 us  [on_device(): pl.pallas_call(functools.partial(kernel, ctx_count, kvh_count, distances)...]
where the time goes in v10:
time: 19.4 us; the launch traced here: 19.2 us
  Pallas kernels  17.9 us (92%)
  between operations  1.29 us (7%)
    pallas_call x1, Pallas kernels, on_device(): pl.pallas_call(functools.partial(kernel, ctx_count, kvh_count, distances)...  17.1 us
    pallas_call x1, Pallas kernels, on_device(): pl.pallas_call(functools.partial(finish, ctx_count, distances), out_shape...  0.86 us

profile of v10, /device:TPU:0, one launch (start us, length us, event | category | flops | bytes accessed | tf_op | source)
XLA Modules:
  0.0 19.2 jit_solution(17708061331599926679)
XLA Ops:
  1.3 17.1 %shard_map.93 = (bf16[128,1024]{1,0:T(8,128)(2,1)S(1)}, bf16[32,4096]{1,0:T(8,128)(2,1)S(1)}, f32[2,64,128]{2,1,0:T(8,128)S(1)}, bf16[2,3,64,128]{3,2,1,0:T(8,128)(2,1)S(1)}, s32[3,8,128]{2,1,0:T(8,128)S(1)}) custom-call(s32[1]{0:T(128)S(6)} %copy.10.cnt_ref, s32[1,8]{1,0:T(1,128)} %sel_hbm.1, bf16[128,1024]{1,0:T(8,128)(2,1)} %q_hbm.1, ...), custom_call_target="tpu_custom_call" | custom-call | tf_op jit(solution)/shard_map/pallas_call | solution.py:341
  18.4 0.9 %shard_map.94 = (bf16[128,1024]{1,0:T(8,128)(2,1)}, bf16[32,4096]{1,0:T(8,128)(2,1)}, f32[128,128]{1,0:T(8,128)}, f32[128,128]{1,0:T(8,128)}) custom-call(bf16[128,1024]{1,0:T(8,128)(2,1)S(1)} %get-tuple-element.9.att, bf16[32,4096]{1,0:T(8,128)(2,1)S(1)} %get-tuple-element.10.gq, f32[2,64,128]{2,1,0:T(8,128)S(1)} %get-tuple-element.11.own, ...), custom_call_target="tpu_custom_call" | custom-call | tf_op jit(solution)/shard_map/pallas_call | solution.py:392
